TPU v7x, 128 devices: a whole 4x4x4 slice. The times are simulated.
128 devices in a mesh: occ: 8 (over z_lo, x), emp: 16 (over z_hi, y, core).
Axes of the slice: x: 4, y: 4, z: 4 (z_hi: 2, z_lo: 2; z = z_hi * 2 + z_lo), core: 2. Of those that a mesh axis runs over, the one named last changes fastest.
Arguments:
- occupied: bfloat16 [2, 32, 96, 9216], P(None, 'occ', 'emp'), may hold values from -5 to 5
- empty: bfloat16 [2, 64, 96, 9216], P(None, 'emp', 'occ'), may hold values from -5 to 5
- occ_energy: float32 [32], P('occ'), may hold values from -0.8 to -0.1
- emp_energy: float32 [64], P('emp'), may hold values from 0.05 to 2
- gvec: int32 [8000], replicated, may hold values from 0 to 15624, as said below
Outputs:
- chi_zero: float32 [2, 8000, 8000], P(None, 'occ', 'emp')
Inputs may be any that keep to these rules, and one draw needn't show every extreme that they name: gvec holds 8000 distinct box indices, those of the 8000 frequencies of smallest length in the box (ties of equal length chosen at random), in a random order.
All inputs are finite; a program needn't handle non-finite values.
Results may differ from a plain program's by a relative error of at most 0.0038.
Values may be sent and summed in bfloat16 or wider, within the bound.
A program may use at most 192 MiB of HBM per device.

v0:
```python
import math

import jax
import jax.numpy as jnp
from jax import lax
from jax.sharding import PartitionSpec as P

GRID = 96
KB = 25


precise = lax.Precision.HIGH


def phase_table(freqs, row_start, row_count):
    freq_index = (jnp.arange(freqs, dtype=jnp.int32) + freqs // 2) % freqs - freqs // 2
    positions = row_start + jnp.arange(row_count, dtype=jnp.int32)
    phases = freq_index[:, None] * positions[None, :] % GRID
    angles = 2.0 * math.pi / GRID * phases.astype(jnp.float32)
    return (jnp.cos(angles), jnp.sin(angles))


def transform(real_in, imag_in, cosine, sine, pattern):
    real_out = jnp.einsum(pattern, real_in, cosine, precision=precise) + jnp.einsum(
        pattern, imag_in, sine, precision=precise
    )
    imag_out = jnp.einsum(pattern, imag_in, cosine, precision=precise) - jnp.einsum(
        pattern, real_in, sine, precision=precise
    )
    return (real_out, imag_out)


def add_rows(totals, occ_rows, emp_rows, block_rows):
    block_count = occ_rows.shape[2] // block_rows
    cos_full, sin_full = phase_table(KB, 0, GRID)

    def one_block(block_no, running):
        offset = block_no * block_rows
        occ_block = lax.dynamic_slice_in_dim(occ_rows, offset, block_rows, 2).astype(jnp.float32)
        emp_block = lax.dynamic_slice_in_dim(emp_rows, offset, block_rows, 2).astype(jnp.float32)
        occ_real = occ_block[0][:, None]
        occ_imag = occ_block[1][:, None]
        emp_real = emp_block[0][None]
        emp_imag = emp_block[1][None]
        pair_count = occ_real.shape[0] * emp_real.shape[1]
        prod_real = (occ_real * emp_real + occ_imag * emp_imag).reshape(
            pair_count, block_rows, GRID, GRID
        )
        prod_imag = (occ_real * emp_imag - occ_imag * emp_real).reshape(
            pair_count, block_rows, GRID, GRID
        )
        zed_real, zed_imag = transform(prod_real, prod_imag, cos_full, sin_full, "pwyz,kz->pwyk")
        why_real, why_imag = transform(zed_real, zed_imag, cos_full, sin_full, "pwyk,jy->pwjk")
        why_real = why_real.reshape(pair_count, block_rows, KB * KB)
        why_imag = why_imag.reshape(pair_count, block_rows, KB * KB)
        cos_rows, sin_rows = phase_table(KB, offset, block_rows)
        ex_real, ex_imag = transform(why_real, why_imag, cos_rows, sin_rows, "pwm,kw->pkm")
        return (running[0] + ex_real, running[1] + ex_imag)

    return lax.fori_loop(0, block_count, one_block, totals)


def contract(left, right):
    return lax.dot_general(
        left, right, (((0,), (0,)), ((), ())), preferred_element_type=jnp.float32
    )


def accumulate(row_side, col_side):
    real_out = contract(row_side[0], col_side[0]) + contract(row_side[1], col_side[1])
    imag_out = contract(row_side[1], col_side[0]) - contract(row_side[0], col_side[1])
    return (real_out, imag_out)


def body(occupied, empty, occ_energy, emp_energy, gvec):
    pair_count = occupied.shape[1] * empty.shape[1]
    zeroes = jnp.zeros((pair_count, KB, KB * KB), jnp.float32)
    whole_empty = lax.all_gather(empty, "occ", axis=2, tiled=True)
    aligned = whole_empty
    spec_real, spec_imag = add_rows(
        (zeroes, zeroes),
        lax.all_gather(occupied, "emp", axis=2, tiled=True),
        aligned,
        occupied.shape[2],
    )
    sphere_real = jnp.take(spec_real.reshape(pair_count, KB**3), gvec, axis=1)
    sphere_imag = jnp.take(spec_imag.reshape(pair_count, KB**3), gvec, axis=1)
    weight = jnp.sqrt(4.0 / (emp_energy[None, :] - occ_energy[:, None])).reshape(
        pair_count, 1
    ) / math.sqrt(GRID**3)
    densities = jnp.stack([sphere_real * weight, sphere_imag * weight]).astype(jnp.bfloat16)
    row_parts = lax.all_to_all(densities, "occ", split_axis=2, concat_axis=1, tiled=True)
    col_parts = lax.all_to_all(densities, "emp", split_axis=2, concat_axis=1, tiled=True)
    n_occ = lax.axis_size("occ")
    n_emp = lax.axis_size("emp")
    col_width = col_parts.shape[2]
    every_col = lax.all_gather(col_parts, "occ", axis=1, tiled=True)
    ordered = (
        every_col.reshape(2, n_occ, n_emp, pair_count, col_width)
        .transpose(0, 2, 1, 3, 4)
        .reshape(2, n_occ * n_emp * pair_count, col_width)
    )
    aligned = ordered
    chi_real, chi_imag = accumulate(lax.all_gather(row_parts, "emp", axis=1, tiled=True), aligned)
    factor = -1.0 / math.sqrt(n_occ * n_emp * pair_count)
    return jnp.stack([chi_real * factor, chi_imag * factor])


def solution(mesh):
    placed = (P(None, "occ", "emp", None), P(None, "emp", "occ", None), P("occ"), P("emp"), P())
    return jax.shard_map(
        body, mesh=mesh, in_specs=placed, out_specs=P(None, "occ", "emp"), check_vma=False
    )
```

profile of v0, /device:TPU:1, one launch (start us, length us, event | category | flops | bytes accessed | tf_op | source)
XLA Modules:
  0.0 1491.2 jit_solution(3041387335170853134)
XLA Ops:
  10.1 148.2 %all-gather.7.cloned.1.call-done = bf16[2,4,96,9216]{3,1,2,0:T(4,128)(2,1)} async-done(((bf16[2,4,12,9216]{3,1,2,0:T(4,128)(2,1)}), bf16[2,4,96,9216]{3,1,2,0:T(4,128)(2,1)}) %all-gather.7.cloned.1.call-update) | async-done | bytes 14155792 | tf_op jit(solution)/shard_map/all_gather | solution.py:78
  158.2 100.0 %all-gather.5.cloned.1.call-done = bf16[2,4,96,9216]{3,1,2,0:T(4,128)(2,1)} async-done(((bf16[2,4,6,9216]{3,1,2,0:T(4,128)(2,1)}), bf16[2,4,96,9216]{3,1,2,0:T(4,128)(2,1)}) %all-gather.5.cloned.1.call-update) | async-done | bytes 14155792 | tf_op jit(solution)/shard_map/all_gather | solution.py:82
  258.2 944.0 %while.22 = (s32[]{:T(128)}, f32[16,25,625]{2,1,0:T(8,128)}, f32[16,25,625]{2,1,0:T(8,128)}, bf16[2,4,96,9216]{3,1,2,0:T(4,128)(2,1)}, bf16[2,4,96,9216]{3,1,2,0...) while((s32[]{:T(128)}, f32[16,25,625]{2,1,0:T(8,128)}, ...), condition=%wide.region_1.2_spmd.clone.clone.clone.clone, body=%wide.region_0.1_spmd.clone.clone.clone.clone.sunk | while | flops 713534016 | bytes 120850400 | solution.py:60
  327.8 8.6 fusion.237
  386.3 8.6 fusion.237
  444.8 8.6 fusion.237
  503.3 8.6 fusion.237
  561.8 8.6 fusion.237
  620.3 8.6 fusion.237
  678.8 8.6 fusion.237
  737.3 8.6 fusion.237
  795.8 8.6 fusion.237
  854.3 8.6 fusion.237
  971.3 8.6 fusion.237
  1146.8 8.6 fusion.237
  1214.1 19.0 %gather_fusion = f32[8000,16]{1,0:T(8,128)} fusion(f32[16,15625]{0,1:T(8,128)} %copy.56, s32[8192]{0:T(1024)S(1)} %copy-done.10), kind=kCustom, calls=%fused_computation.clone | custom fusion | bytes 1056000 | tf_op jit(solution)/shard_map/jit(_take)/gather | solution.py:86
  1233.1 19.1 %gather_fusion.1 = f32[8000,16]{1,0:T(8,128)} fusion(f32[16,15625]{0,1:T(8,128)} %copy.57, s32[8192]{0:T(1024)S(1)} %copy-done.10), kind=kCustom, calls=%fused_computation.1.clone | custom fusion | bytes 1056000 | tf_op jit(solution)/shard_map/jit(_take)/gather | solution.py:87
  1259.8 34.6 %copy.88 = bf16[2,16,8000]{1,0,2:T(2,128)(2,1)} copy(bf16[2,16,8000]{1,2,0:T(8,128)(2,1)S(1)} %pad_maximum_fusion) | data formatting | bytes 1024000 | tf_op jit(solution)/shard_map/stack | solution.py:91
  1300.0 14.1 all_to_all.36
  1318.2 10.3 copy.67
  1328.6 29.6 %copy.89 = bf16[2,16,8000]{1,0,2:T(2,128)(2,1)} copy(bf16[2,16,8000]{1,2,0:T(8,128)(2,1)} %copy-done.8) | data formatting | bytes 1024000 | tf_op jit(solution)/shard_map/stack | solution.py:91
  1364.1 17.3 %all_to_all.37 = bf16[8,2,16000]{2,1,0:T(2,128)(2,1)S(1)} all-to-all(bf16[8,2,16000]{2,1,0:T(2,128)(2,1)S(1)} %reshape.191), channel_id=1, replica_groups=mesh['occ'=8,'emp'=16] {'occ'}, dimensions={0} | all-to-all | bytes 1024000 | tf_op jit(solution)/shard_map/all_to_all | solution.py:92
  1386.4 10.3 copy.59
  1401.1 68.4 %all-gather.9.cloned.1.call-done = bf16[2,2048,1000]{2,1,0:T(8,128)(2,1)} async-done(((bf16[2,128,1000]{2,1,0:T(8,128)(2,1)}), bf16[2,2048,1000]{2,1,0:T(8,128)(2,1)}) %all-gather.9.cloned.1.call-update) | async-done | bytes 8192016 | tf_op jit(solution)/shard_map/all_gather | solution.py:104
  (650 shorter events, 893.2 us)
Async XLA Ops:
  6.5 151.7 %all-gather.7.cloned.1.call-start = ((), (), s32[]{:S(2)}) async-start(), calls=%async_computation.3 | async-start | bytes 15925248 | tf_op jit(solution)/shard_map/all_gather | solution.py:78
  7.3 250.9 %all-gather.5.cloned.1.call-start = ((), (), s32[]{:S(2)}) async-start(), calls=%async_computation.2 | async-start | bytes 15040512 | tf_op jit(solution)/shard_map/all_gather | solution.py:82
  8.0 1388.6 %all-gather.11.cloned.1.call-start = ((), (), s32[]{:S(2)}) async-start(), calls=%async_computation.5 | async-start | bytes 4718592 | tf_op jit(solution)/shard_map/all_gather | solution.py:97
  269.3 8.6 copy-start.1
  288.2 8.0 copy-start.2
  327.8 8.6 copy-start.1
  386.3 8.6 copy-start.1
  444.8 8.6 copy-start.1
  503.3 8.6 copy-start.1
  561.8 8.6 copy-start.1
  620.3 8.6 copy-start.1
  678.8 8.6 copy-start.1
  737.3 8.6 copy-start.1
  795.8 8.6 copy-start.1
  854.3 8.6 copy-start.1
  912.8 8.6 copy-start.1
  971.3 8.6 copy-start.1
  1029.8 8.6 copy-start.1
  1088.3 8.6 copy-start.1
  1146.8 8.6 copy-start.1
  1233.1 19.1 %copy-start.12 = (pred[8000]{0:T(1024)(128)(4,1)S(1)}, pred[8000]{0:T(1024)(128)(4,1)}, u32[]{:S(2)}) copy-start(pred[8000]{0:T(1024)(128)(4,1)} %compare_and_fusion) | copy-start | bytes 24004
  1233.1 19.1 %copy-start.13 = (f32[16]{0:T(128)S(1)}, f32[16]{0:T(128)}, u32[]{:S(2)}) copy-start(f32[16]{0:T(128)} %div.16) | copy-start | bytes 196
  1259.8 34.6 %copy-start.8 = (bf16[2,16,8000]{1,2,0:T(8,128)(2,1)}, bf16[2,16,8000]{1,2,0:T(8,128)(2,1)S(1)}, u32[]{:S(2)}) copy-start(bf16[2,16,8000]{1,2,0:T(8,128)(2,1)S(1)} %pad_maximum_fusion) | copy-start | bytes 1536004
  1328.5 141.0 %all-gather.9.cloned.1.call-start = ((), (), s32[]{:S(2)}) async-start(), calls=%async_computation.4 | async-start | bytes 8912896 | tf_op jit(solution)/shard_map/all_gather | solution.py:104
  (102 other events, 376.2 us)
Sparse Core Ops, SparseCore 0:
  9.0 149.1 all-gather.6
  160.7 97.4 all-gather.4
  1328.7 55.6 all-gather.10
  1396.8 72.7 all-gather.8
where the time goes:
time: 1510 us; the launch traced here: 1490 us
  matrix products  578 us (38%)
  local copies, waits for them, and re-layouts  448 us (30%)
  waiting for transfers between devices  318 us (21%)
  other arithmetic  90.9 us (6%)
  blocking collectives  31.4 us (2%)
    dot_general x48, matrix products, transform(): jnp.einsum(pattern, imag_in, cosine, precision=precise)  166 us
    dot_general x48, matrix products, transform(): jnp.einsum(pattern, real_in, sine, precision=precise)  162 us
    all_gather x1, waiting for transfers between devices, body(): whole_empty = lax.all_gather(empty, 'occ', axis=2, tiled=True)  148 us
    dot_general x48, matrix products, transform(): jnp.einsum(pattern, imag_in, sine, precision=precise)  132 us
    dot_general x48, matrix products, transform(): jnp.einsum(pattern, real_in, cosine, precision=precise)  107 us
    all_gather x1, waiting for transfers between devices, body(): lax.all_gather(occupied, 'emp', axis=2, tiled=True)  100 us
    sub x16, local copies, waits for them, and re-layouts, one_block(): occ_real * emp_imag - occ_imag * emp_real  93.1 us
    reshape x32, local copies, waits for them, and re-layouts, one_block(): why_imag = why_imag.reshape(pair_count, block_rows, KB * KB)  69.3 us
  transfers between devices with their start and end apart: 4, of which 3 were waited for; matrix products, arithmetic and copies ran while one was open for 4% of the time, Pallas kernels for 0%

commit v1 on v0

v1 whole, which is shorter than its diff:
```python
import functools
import math

import jax
import jax.numpy as jnp
import ml_dtypes
import numpy as np
from jax import lax
from jax.experimental import pallas as pl
from jax.experimental.pallas import tpu as pltpu
from jax.sharding import PartitionSpec as P

GRID = 96
KB = 25
REACH = KB // 2
NG = 8000
RSQ = 153
GROUPS = 24
HALF = 256
KZ = 32
BLOCK = 500
BLOCK_PAD = 512

f32 = jnp.float32
bf16 = jnp.bfloat16


def split(table):
    high = table.astype(ml_dtypes.bfloat16)
    low = (table - high.astype(np.float64)).astype(ml_dtypes.bfloat16)
    return high, low


def half_disc():
    kept = []
    for kx in range(-REACH, REACH + 1):
        for ky in range(-REACH, REACH + 1):
            if kx * kx + ky * ky <= RSQ and (kx > 0 or (kx == 0 and ky >= 0)):
                kept.append((kx, ky))
    return np.array(kept)


def tables():
    theta = 2.0 * np.pi / GRID
    disc = half_disc()
    kx, ky = disc[:, 0], disc[:, 1]
    freq = (np.arange(KB) + REACH) % KB - REACH
    angle = theta * (np.outer(np.arange(GRID), freq) % GRID)
    first = np.zeros((2, 4, GRID, 2, 4, KZ))
    for y in range(4):
        first[0, y, :, 0, y, :KB] = np.cos(angle)
        first[0, y, :, 1, y, :KB] = -np.sin(angle)
        first[1, y, :, 0, y, :KB] = np.sin(angle)
        first[1, y, :, 1, y, :KB] = np.cos(angle)
    first = first.reshape(768, 256)
    j = np.repeat(np.arange(GROUPS), GRID)
    x = np.tile(np.arange(GRID), GROUPS)
    angle = theta * ((np.outer(kx, x) + 4 * np.outer(ky, j)) % GRID)
    second = np.zeros((2, HALF, GROUPS * GRID))
    second[0, : len(disc)] = np.cos(angle)
    second[1, : len(disc)] = np.sin(angle)
    second = second.reshape(2 * HALF, GROUPS * GRID)
    angle = theta * ((ky[:, None] * np.repeat(np.arange(4), KZ)[None, :]) % GRID)
    twiddle = np.zeros((2, HALF, 4 * KZ), np.float32)
    twiddle[0, : len(disc)] = np.cos(angle)
    twiddle[1, : len(disc)] = np.sin(angle)
    column = np.full((2, HALF), -1, np.int32)
    column[0, : len(disc)] = (kx % KB) * KB + ky % KB
    column[1, 1 : len(disc)] = ((-kx) % KB)[1:] * KB + ((-ky) % KB)[1:]
    return split(first), split(second), twiddle, column.reshape(2 * HALF, 1)


def pair_kernel(weight, occ, emp, t_hi, t_lo, a_hi, a_lo, tw, out, z_hi, z_lo):
    n_occ = occ.shape[1]
    c = pl.program_id(0)
    tile = 4

    def one_band(v, carry):
        def one_tile(jt, carry2):
            res = []
            ims = []
            for jj in range(tile):
                for q in range(3):
                    lanes = pl.ds(pl.multiple_of((jt * tile + jj) * 384 + q * 128, 128), 128)
                    vr = occ[0, v, :, lanes].astype(f32)
                    vi = occ[1, v, :, lanes].astype(f32)
                    cr = emp[0, 0, :, lanes].astype(f32)
                    ci = emp[1, 0, :, lanes].astype(f32)
                    res.append(vr * cr + vi * ci)
                    ims.append(vr * ci - vi * cr)
            rows = []
            rows_lo = []
            for jj in range(tile):
                parts = res[3 * jj : 3 * jj + 3] + ims[3 * jj : 3 * jj + 3]
                high = [p.astype(bf16) for p in parts]
                low = [(p - h.astype(f32)).astype(bf16) for p, h in zip(parts, high)]
                rows.append(jnp.concatenate(high, axis=1))
                rows_lo.append(jnp.concatenate(low, axis=1))
            high = jnp.concatenate(rows, axis=0)
            low = jnp.concatenate(rows_lo, axis=0)
            z = (
                jnp.dot(high, t_hi[...], preferred_element_type=f32)
                + jnp.dot(low, t_hi[...], preferred_element_type=f32)
                + jnp.dot(high, t_lo[...], preferred_element_type=f32)
            )
            zh = z.astype(bf16)
            where = pl.ds(pl.multiple_of(jt * (tile * GRID), 128), tile * GRID)
            z_hi[where, :] = zh
            z_lo[where, :] = (z - zh.astype(f32)).astype(bf16)
            return carry2

        lax.fori_loop(0, GROUPS // tile, one_tile, 0)
        both = (
            jnp.dot(a_hi[...], z_hi[...], preferred_element_type=f32)
            + jnp.dot(a_hi[...], z_lo[...], preferred_element_type=f32)
            + jnp.dot(a_lo[...], z_hi[...], preferred_element_type=f32)
        )
        ur = both[:HALF, :128]
        ui = both[:HALF, 128:]
        wr = both[HALF:, :128]
        wi = both[HALF:, 128:]
        cos, sin = tw[0], tw[1]
        w = weight[v, c]
        for sign in range(2):
            s = 1.0 - 2.0 * sign
            pr = ur + s * wi
            pi = ui - s * wr
            qr = (cos * pr + s * (sin * pi)).T
            qi = (cos * pi - s * (sin * pr)).T
            for at, q in ((0, qr), (1, qi)):
                total = (q[:KZ] + q[KZ : 2 * KZ]) + (q[2 * KZ : 3 * KZ] + q[3 * KZ :])
                out[at, v, 0, :, sign * HALF : (sign + 1) * HALF] = (total * w).astype(bf16)
        return carry

    lax.fori_loop(0, n_occ, one_band, 0)


def compact(weight, occ_all, emp_all):
    (t_hi, t_lo), (a_hi, a_lo), tw, unused = tables()
    n_occ, n_emp = occ_all.shape[1], emp_all.shape[1]
    whole = lambda shape: pl.BlockSpec(shape, lambda c: (0,) * len(shape), pipeline_mode=pl.Buffered(1))
    return pl.pallas_call(
        pair_kernel,
        grid=(n_emp,),
        out_shape=jax.ShapeDtypeStruct((2, n_occ, n_emp, KZ, 2 * HALF), bf16),
        in_specs=[
            pl.BlockSpec(memory_space=pltpu.SMEM),
            whole((2, n_occ, GRID, GRID * GRID)),
            pl.BlockSpec((2, 1, GRID, GRID * GRID), lambda c: (0, c, 0, 0)),
            whole((768, 256)),
            whole((768, 256)),
            whole((2 * HALF, GROUPS * GRID)),
            whole((2 * HALF, GROUPS * GRID)),
            whole((2, HALF, 128)),
        ],
        out_specs=pl.BlockSpec((2, n_occ, 1, KZ, 2 * HALF), lambda c: (0, 0, c, 0, 0)),
        scratch_shapes=[
            pltpu.VMEM((GROUPS * GRID, 256), bf16),
            pltpu.VMEM((GROUPS * GRID, 256), bf16),
        ],
        compiler_params=pltpu.CompilerParams(vmem_limit_bytes=58 * 2**20),
        name="pair_spectra",
    )(weight, occ_all, emp_all, t_hi, t_lo, a_hi, a_lo, tw)


def select_kernel(column, kxy, kz, x, out):
    hot = jnp.where(column[...] == kxy[0], 1.0, 0.0).astype(bf16)
    rows = x.shape[0] // KZ
    picked = jnp.dot(x[...], hot, preferred_element_type=f32)
    level = lax.broadcasted_iota(jnp.int32, (KZ, BLOCK_PAD), 0)
    mask = jnp.where(level == kz[0], 1.0, 0.0)
    total = jnp.sum(picked.reshape(rows, KZ, BLOCK_PAD) * mask[None], axis=1)
    out[0] = total.astype(bf16)


def select(gvec, x):
    column = tables()[3]
    blocks = NG // BLOCK
    padded = jnp.pad(gvec.reshape(blocks, 1, BLOCK), ((0, 0), (0, 0), (0, BLOCK_PAD - BLOCK)), constant_values=0)
    kxy = padded // KB
    kz = padded - kxy * KB
    live = lax.broadcasted_iota(jnp.int32, padded.shape, 2) < BLOCK
    kxy = jnp.where(live, kxy, -2)
    rows = x.shape[0] // KZ
    return pl.pallas_call(
        select_kernel,
        grid=(blocks,),
        out_shape=jax.ShapeDtypeStruct((blocks, rows, BLOCK_PAD), bf16),
        in_specs=[
            pl.BlockSpec((2 * HALF, 1), lambda b: (0, 0)),
            pl.BlockSpec((1, 1, BLOCK_PAD), lambda b: (b, 0, 0)),
            pl.BlockSpec((1, 1, BLOCK_PAD), lambda b: (b, 0, 0)),
            pl.BlockSpec(x.shape, lambda b: (0, 0)),
        ],
        out_specs=pl.BlockSpec((1, rows, BLOCK_PAD), lambda b: (b, 0, 0)),
        compiler_params=pltpu.CompilerParams(vmem_limit_bytes=40 * 2**20),
        name="sphere_select",
    )(column, kxy, kz, x)


def densities_of(occ_all, emp_all, occ_energy, emp_energy, gvec):
    weight = jnp.sqrt(4.0 / (emp_energy[None, :] - occ_energy[:, None])) / math.sqrt(GRID**3)
    x = compact(weight, occ_all, emp_all)
    rows = 2 * x.shape[1] * x.shape[2]
    return select(gvec, x.reshape(rows * KZ, 2 * HALF))


def body(occupied, empty, occ_energy, emp_energy, gvec):
    emp_all = lax.all_gather(empty, "occ", axis=2, tiled=True)
    occ_all = lax.all_gather(occupied, "emp", axis=2, tiled=True)
    d = densities_of(occ_all, emp_all, occ_energy, emp_energy, gvec)
    n_occ = lax.axis_size("occ")
    n_emp = lax.axis_size("emp")
    rows = d.shape[1]
    r = d.reshape(n_occ, 1, 2, rows, BLOCK_PAD)
    r = lax.all_to_all(r, "occ", split_axis=0, concat_axis=1, tiled=False) if False else lax.all_to_all(
        d.reshape(n_occ, 2, rows, BLOCK_PAD), "occ", split_axis=0, concat_axis=0, tiled=True
    )
    r = lax.all_gather(r, "emp", axis=0)
    c = lax.all_to_all(d, "emp", split_axis=0, concat_axis=0, tiled=True)
    c = lax.all_gather(c, "occ", axis=0)
    c = c.transpose(1, 0, 2, 3)
    half = rows // 2
    count = n_occ * n_emp * half
    factor = -1.0 / math.sqrt(count)
    cr, ci = c[:, :, :half], c[:, :, half:]
    turned = jnp.concatenate([-ci, cr], axis=2)
    dims = (((0, 1, 2), (0, 1, 2)), ((), ()))
    left = r.transpose(0, 1, 3, 2, 4)
    real = lax.dot_general(left, c, dims, preferred_element_type=f32)
    imag = lax.dot_general(left, turned, dims, preferred_element_type=f32)

    def trim(a):
        return (a * factor)[:, :BLOCK, :BLOCK].reshape(2 * BLOCK, BLOCK)

    return jnp.stack([trim(real), trim(imag)])


def solution(mesh):
    placed = (P(None, "occ", "emp", None), P(None, "emp", "occ", None), P("occ"), P("emp"), P())
    return jax.shard_map(
        body, mesh=mesh, in_specs=placed, out_specs=P(None, "occ", "emp"), check_vma=False
    )
```

time: 1510 us -> 584 us (0.39); the launches traced: 1490 us -> 583 us
  matrix products: 578 us -> 15.1 us
  local copies, waits for them, and re-layouts: 448 us -> 36.1 us
  Pallas kernels: 0 us -> 139 us
  other arithmetic: 90.9 us -> 9.17 us
  waiting for transfers between devices: 318 us -> 341 us
    dot_general x196 -> x2, matrix products: 578 us -> 15.1 us  [the longest x1 10.6 us: body(): real = lax.dot_general(left, c, dims, preferred_element_type=f32)]
    pallas_call x0 -> x2, Pallas kernels: none -> 139 us  [the longest x1 126 us: compact(): pl.pallas_call(pair_kernel, grid=(n_emp,), out_shape=jax.ShapeDtypeStruct...]
    reshape x69 -> x1, local copies, waits for them, and re-layouts: 113 us -> 0.12 us  [select(): gvec.reshape(blocks, 1, BLOCK)]
    sub x16 -> x0, local copies, waits for them, and re-layouts: 93.1 us -> none  [one_block(): occ_real * emp_imag - occ_imag * emp_real]
    add x16 -> x0, local copies, waits for them, and re-layouts: 67.1 us -> none  [one_block(): occ_real * emp_real + occ_imag * emp_imag]
    another operation x2, local copies, waits for them, and re-layouts: 64.2 us -> 3.06 us  [body(): return jnp.stack([trim(real), trim(imag)])]
    add x32 -> x0, other arithmetic: 50 us -> none  [the longest x16 50 us: one_block(): occ_real * emp_real + occ_imag * emp_imag]
    gather x2 -> x0, local copies, waits for them, and re-layouts: 38.1 us -> none  [the longest x1 19.1 us: body(): sphere_imag = jnp.take(spec_imag.reshape(pair_count, KB ** 3), gvec, axis=1)]
  transfers between devices with their start and end apart: 4 -> 4, of which waited for: 3 -> 4; matrix products, arithmetic and copies ran while one was open for 4% -> 3% of each run, Pallas kernels for 0% -> 0%
where the time goes in v1:
time: 584 us; the launch traced here: 583 us
  waiting for transfers between devices  341 us (58%)
  Pallas kernels  139 us (24%)
  local copies, waits for them, and re-layouts  36.1 us (6%)
  blocking collectives  30.3 us (5%)
  matrix products  15.1 us (3%)
  between operations  13.2 us (2%)
  other arithmetic  9.17 us (2%)
    all_gather x1, waiting for transfers between devices, body(): emp_all = lax.all_gather(empty, 'occ', axis=2, tiled=True)  147 us
    pallas_call x1, Pallas kernels, compact(): pl.pallas_call(pair_kernel, grid=(n_emp,), out_shape=jax.ShapeDtypeStruct...  126 us
    all_gather x1, waiting for transfers between devices, body(): occ_all = lax.all_gather(occupied, 'emp', axis=2, tiled=True)  87.8 us
    all_gather x1, waiting for transfers between devices, body(): r = lax.all_gather(r, 'emp', axis=0)  66.8 us
    all_gather x1, waiting for transfers between devices, body(): c = lax.all_gather(c, 'occ', axis=0)  39 us
    all_to_all x1, blocking collectives, body(): lax.all_to_all(d.reshape(n_occ, 2, rows, BLOCK_PAD), 'occ', split_axis=0,...  15.5 us
    all_to_all x1, blocking collectives, body(): c = lax.all_to_all(d, 'emp', split_axis=0, concat_axis=0, tiled=True)  14.8 us
    pallas_call x1, Pallas kernels, select(): pl.pallas_call(select_kernel, grid=(blocks,), out_shape=jax.ShapeDtypeStr...  12.8 us
  transfers between devices with their start and end apart: 4, of which 4 were waited for; matrix products, arithmetic and copies ran while one was open for 3% of the time, Pallas kernels for 0%

profile of v1, /device:TPU:1, one launch (start us, length us, event | category | flops | bytes accessed | tf_op | source)
XLA Modules:
  0.0 583.4 jit_solution(2494514181495747608)
XLA Ops:
  6.6 3.5 copy.25
  10.2 1.3 copy.24
  11.7 0.2 multiply_subtract_fusion
  11.9 0.7 sqrt_multiply_fusion.weight
  12.6 146.9 %all-gather.9.cloned.1.call-done = bf16[2,4,96,9216]{3,1,0,2:T(4,128)(2,1)} async-done(((bf16[2,4,12,9216]{3,1,0,2:T(4,128)(2,1)}), bf16[2,4,96,9216]{3,1,0,2:T(4,128)(2,1)}) %all-gather.9.cloned.1.call-update) | async-done | bytes 14155792 | tf_op jit(solution)/shard_map/all_gather | solution.py:209
  159.5 12.1 %copy.27.emp = bf16[2,4,96,9216]{3,2,1,0:T(8,128)(2,1)} copy(bf16[2,4,96,9216]{3,1,0,2:T(4,128)(2,1)} %all-gather.9.cloned.1.call-done) | data formatting | bytes 28311552 | tf_op jit(solution)/shard_map/all_gather | solution.py:209
  171.6 87.8 %all-gather.7.cloned.1.call-done = bf16[2,4,96,9216]{3,1,0,2:T(4,128)(2,1)} async-done(((bf16[2,4,6,9216]{3,1,0,2:T(4,128)(2,1)}), bf16[2,4,96,9216]{3,1,0,2:T(4,128)(2,1)}) %all-gather.7.cloned.1.call-update) | async-done | bytes 14155792 | tf_op jit(solution)/shard_map/all_gather | solution.py:210
  259.4 12.2 %copy.26.occ = bf16[2,4,96,9216]{3,2,1,0:T(8,128)(2,1)} copy(bf16[2,4,96,9216]{3,1,0,2:T(4,128)(2,1)} %all-gather.7.cloned.1.call-done) | data formatting | bytes 28311552 | tf_op jit(solution)/shard_map/all_gather | solution.py:210
  271.5 126.0 %pair_spectra.1 = bf16[2,4,4,32,512]{4,3,2,1,0:T(8,128)(2,1)} custom-call(f32[4,4]{1,0:T(4,128)} %sqrt_multiply_fusion.weight, bf16[2,4,96,9216]{3,2,1,0:T(8,128)(2,1)} %copy.26.occ, bf16[2,4,96,9216]{3,2,1,0:T(8,128)(2,1)} %copy.27.emp, bf16[768,256]{1,0:T(8,128)(2,1)} %constant.36.clone.t_hi, bf16[768,256]{1,0:T(8,128)(2,1)} %constant.37.clone.t_lo, ...), custom_call_target="tpu_custom_call" | custom-call | tf_op jit(solution)/shard_map/pair_spectra/pallas_call | solution.py:142
  397.5 1.2 copy-done
  398.7 12.8 %sphere_select.1 = bf16[16,32,512]{2,1,0:T(8,128)(2,1)S(1)} custom-call(s32[512,1]{1,0:T(8,128)S(1)} %copy-done.1, s32[16,1,512]{2,1,0:T(1,128)S(1)} %broadcast_select_fusion.kxy, s32[16,1,512]{2,1,0:T(1,128)S(1)} %get-tuple-element.5.kz, bf16[1024,512]{1,0:T(8,128)(2,1)S(1)} %bitcast.40), custom_call_target="tpu_custom_call" | custom-call | tf_op jit(solution)/shard_map/sphere_select/pallas_call | solution.py:185
  411.6 14.8 %all_to_all.10 = bf16[16,32,512]{2,1,0:T(8,128)(2,1)} all-to-all(bf16[16,32,512]{2,1,0:T(8,128)(2,1)S(1)} %sphere_select.1), channel_id=1, replica_groups=mesh['occ'=8,'emp'=16] {'emp'}, dimensions={0} | all-to-all | bytes 1048576 | tf_op jit(solution)/shard_map/all_to_all | solution.py:220
  426.5 15.5 %all_to_all.11 = bf16[8,2,32,512]{3,2,1,0:T(8,128)(2,1)} all-to-all(bf16[8,2,32,512]{3,2,1,0:T(8,128)(2,1)S(1)} %bitcast.39), channel_id=1, replica_groups=mesh['occ'=8,'emp'=16] {'occ'}, dimensions={0} | all-to-all | bytes 1048576 | tf_op jit(solution)/shard_map/all_to_all | solution.py:216
  442.0 39.0 %all-gather.13.cloned.1.call-done = bf16[128,32,512]{2,1,0:T(8,128)(2,1)} async-done(((bf16[16,32,512]{2,1,0:T(8,128)(2,1)}), bf16[128,32,512]{2,1,0:T(8,128)(2,1)}) %all-gather.13.cloned.1.call-update) | async-done | bytes 4194320 | tf_op jit(solution)/shard_map/all_gather | solution.py:221
  480.9 2.7 copy.53
  483.6 1.6 slice_negate_fusion
  485.2 66.8 %all-gather.11.cloned.1.call-done = bf16[128,2,32,512]{3,2,1,0:T(8,128)(2,1)} async-done(((bf16[8,2,32,512]{3,2,1,0:T(8,128)(2,1)}), bf16[128,2,32,512]{3,2,1,0:T(8,128)(2,1)}) %all-gather.11.cloned.1.call-update) | async-done | bytes 8388624 | tf_op jit(solution)/shard_map/all_gather | solution.py:219
  552.1 10.6 %fusion.10 = f32[2,512,512]{2,1,0:T(8,128)} fusion(bf16[8,16,32,512]{3,2,1,0:T(8,128)(2,1)} %bitcast.43, bf16[16,8,2,32,512]{4,3,2,1,0:T(8,128)(2,1)} %bitcast.44), kind=kOutput, calls=%fused_computation.16 | convolution fusion | flops 4294967296 | bytes 14680064 | tf_op jit(solution)/shard_map/dot_general | solution.py:230
  562.6 4.5 fusion.15
  567.2 0.2 slice_multiply_fusion
  567.4 1.5 stack_reshape.7
  569.0 1.8 slice_multiply_fusion.1
  570.8 1.5 stack_reshape.6
  572.3 4.6 pad_maximum_fusion
  (26 shorter events, 0.4 us)
Async XLA Ops:
  6.5 3.6 copy-start.3
  6.5 5.0 copy-start.4
  6.5 5.3 copy-start.5
  6.5 5.3 copy-start.6
  6.5 152.9 %all-gather.9.cloned.1.call-start = ((), (), s32[]{:S(2)}) async-start(), calls=%async_computation.3 | async-start | bytes 15925248 | tf_op jit(solution)/shard_map/all_gather | solution.py:209
  10.1 249.3 %all-gather.7.cloned.1.call-start = ((), (), s32[]{:S(2)}) async-start(), calls=%async_computation.2 | async-start | bytes 15040512 | tf_op jit(solution)/shard_map/all_gather | solution.py:210
  11.5 469.5 %all-gather.13.cloned.1.call-start = ((), (), s32[]{:S(2)}) async-start(), calls=%async_computation.5 | async-start | bytes 4718592 | tf_op jit(solution)/shard_map/all_gather | solution.py:221
  271.5 126.0 %copy-start.1 = (s32[512,1]{1,0:T(8,128)S(1)}, s32[512,1]{1,0:T(8,128)}, u32[]{:S(2)}) copy-start(s32[512,1]{1,0:T(8,128)} %constant.41.clone.column) | copy-start | bytes 6148
  397.5 1.2 copy-start
  426.4 125.6 %all-gather.11.cloned.1.call-start = ((), (), s32[]{:S(2)}) async-start(), calls=%async_computation.4 | async-start | bytes 8912896 | tf_op jit(solution)/shard_map/all_gather | solution.py:219
  552.1 10.6 %copy-start.2 = (bf16[16,8,16,512]{3,2,1,0:T(8,128)(2,1)S(1)}, bf16[16,8,16,512]{3,2,1,0:T(8,128)(2,1)}, u32[]{:S(2)}) copy-start(bf16[16,8,16,512]{3,2,1,0:T(8,128)(2,1)} %get-tuple-element.8) | copy-start | bytes 6291460
  552.1 10.6 %copy-start.7 = (bf16[128,2,32,512]{3,2,1,0:T(8,128)(2,1)S(1)}, bf16[128,2,32,512]{3,2,1,0:T(8,128)(2,1)}, u32[]{:S(2)}) copy-start(bf16[128,2,32,512]{3,2,1,0:T(8,128)(2,1)} %all-gather.11.cloned.1.call-done) | copy-start | bytes 25165828
Sparse Core Ops, SparseCore 0:
  10.2 149.1 all-gather.8
  161.9 97.4 all-gather.6
  426.5 54.3 all-gather.12
  483.2 68.7 all-gather.10

commit v2 on v1

--- a/solution.py
+++ b/solution.py
@@ -16,6 +16,8 @@
 NG = 8000
 RSQ = 153
 GROUPS = 24
+SLAB = 6
+ROWS = GROUPS * SLAB
 HALF = 256
 KZ = 32
 BLOCK = 500
@@ -53,8 +55,8 @@
         first[1, y, :, 0, y, :KB] = np.sin(angle)
         first[1, y, :, 1, y, :KB] = np.cos(angle)
     first = first.reshape(768, 256)
-    j = np.repeat(np.arange(GROUPS), GRID)
-    x = np.tile(np.arange(GRID), GROUPS)
+    half, slab, j, x = [a.reshape(-1) for a in np.meshgrid(*map(np.arange, (2, 8, GROUPS, SLAB)), indexing="ij")]
+    x = 2 * SLAB * slab + SLAB * half + x
     angle = theta * ((np.outer(kx, x) + 4 * np.outer(ky, j)) % GRID)
     second = np.zeros((2, HALF, GROUPS * GRID))
     second[0, : len(disc)] = np.cos(angle)
@@ -70,46 +72,237 @@
     return split(first), split(second), twiddle, column.reshape(2 * HALF, 1)
 
 
-def pair_kernel(weight, occ, emp, t_hi, t_lo, a_hi, a_lo, tw, out, z_hi, z_lo):
-    n_occ = occ.shape[1]
-    c = pl.program_id(0)
-    tile = 4
-
-    def one_band(v, carry):
-        def one_tile(jt, carry2):
-            res = []
-            ims = []
-            for jj in range(tile):
+MESH = pl.DeviceIdType.MESH
+KINDS = 9
+
+
+def gather_steps(send, recv, shard, piece, hi, ring, device_of):
+    own = hi * 4 + ring
+    mate = (1 - hi) * 4 + ring
+    right, left, far = lax.rem(ring + 1, 4), lax.rem(ring + 3, 4), lax.rem(ring + 2, 4)
+
+    def copy(kind, ref, target):
+        return pltpu.make_async_remote_copy(
+            src_ref=ref,
+            dst_ref=ref,
+            send_sem=send.at[kind],
+            recv_sem=recv.at[kind],
+            device_id=device_of(target),
+            device_id_type=MESH,
+        )
+
+    to_right, to_left = hi * 4 + right, hi * 4 + left
+    from_left, from_right, across = hi * 4 + left, hi * 4 + right, hi * 4 + far
+    mate_left, mate_right, mate_across = (1 - hi) * 4 + left, (1 - hi) * 4 + right, (1 - hi) * 4 + far
+
+    sends = [
+        (0, shard(own), mate),
+        (1, shard(own), to_right),
+        (2, shard(own), to_left),
+        (3, shard(mate), to_right),
+        (4, shard(mate), to_left),
+        (5, piece(from_left, 0), to_right),
+        (6, piece(from_right, 1), to_left),
+        (7, piece(mate_left, 0), to_right),
+        (8, piece(mate_right, 1), to_left),
+    ]
+    landings = [
+        shard(mate),
+        shard(from_left),
+        shard(from_right),
+        shard(mate_left),
+        shard(mate_right),
+        piece(across, 0),
+        piece(across, 1),
+        piece(mate_across, 0),
+        piece(mate_across, 1),
+    ]
+
+    def start(*kinds):
+        for kind in kinds:
+            copy(*sends[kind]).start()
+
+    def arrived(*kinds):
+        for kind in kinds:
+            copy(kind, landings[kind], own).wait_recv()
+
+    def begin():
+        start(0, 1, 2)
+
+    def mid():
+        arrived(0)
+        start(3, 4)
+        arrived(1)
+        start(5)
+        arrived(2)
+        start(6)
+
+    def late():
+        arrived(3)
+        start(7)
+        arrived(4)
+        start(8)
+
+    def finish():
+        arrived(5, 6, 7, 8)
+
+    def sent():
+        for kind in range(KINDS):
+            copy(*sends[kind]).wait_send()
+
+    return begin, mid, late, finish, sent
+
+
+def pair_kernel(
+    weight, occ_in, emp_in, t_hi, t_lo, a_hi, a_lo, tw, out,
+    occ, emp, z_hi, z_lo, local, o_send, o_recv, e_send, e_recv, s_send, s_recv,
+):
+    n_occ, n_emp = occ.shape[0], emp.shape[0]
+    o = lax.axis_index("occ")
+    m = lax.axis_index("emp")
+    o_hi, o_ring = o // 4, lax.rem(o, 4)
+    chip, core = m // 2, lax.rem(m, 2)
+    c_hi, c_ring = chip // 4, lax.rem(chip, 4)
+
+    def emp_band(c):
+        return gather_steps(
+            e_send.at[c], e_recv.at[c],
+            lambda i: emp.at[c, :, i],
+            lambda i, h: emp.at[c, h, i],
+            o_hi, o_ring,
+            lambda i: {"occ": i, "emp": m},
+        )
+
+    def occ_band(v):
+        return gather_steps(
+            o_send.at[v], o_recv.at[v],
+            lambda i: occ.at[v, core, i],
+            lambda i, h: occ.at[v, core, i, h],
+            c_hi, c_ring,
+            lambda i: {"occ": o, "emp": 2 * i + core},
+        )
+
+    sibling = {"occ": o, "emp": 2 * chip + 1 - core}
+
+    def share(v, mine):
+        return pltpu.make_async_remote_copy(
+            src_ref=occ.at[v, mine],
+            dst_ref=occ.at[v, mine],
+            send_sem=s_send.at[v],
+            recv_sem=s_recv.at[v],
+            device_id=sibling,
+            device_id_type=MESH,
+        )
+
+    copies = []
+    for v in range(n_occ):
+        copies.append(pltpu.make_async_copy(occ_in.at[v], occ.at[v, core, chip], local.at[v]))
+    for c in range(n_emp):
+        copies.append(pltpu.make_async_copy(emp_in.at[c], emp.at[c, :, o], local.at[n_occ + c]))
+    for copy in copies:
+        copy.start()
+
+    barrier = pltpu.get_barrier_semaphore()
+    peers = [
+        {"occ": (1 - o_hi) * 4 + o_ring, "emp": m},
+        {"occ": o_hi * 4 + lax.rem(o_ring + 1, 4), "emp": m},
+        {"occ": o_hi * 4 + lax.rem(o_ring + 3, 4), "emp": m},
+        {"occ": o, "emp": 2 * ((1 - c_hi) * 4 + c_ring) + core},
+        {"occ": o, "emp": 2 * (c_hi * 4 + lax.rem(c_ring + 1, 4)) + core},
+        {"occ": o, "emp": 2 * (c_hi * 4 + lax.rem(c_ring + 3, 4)) + core},
+        sibling,
+    ]
+    for peer in peers:
+        pl.semaphore_signal(barrier, inc=1, device_id=peer, device_id_type=MESH)
+    pl.semaphore_wait(barrier, len(peers))
+    for copy in copies:
+        copy.wait()
+
+    E = [emp_band(c) for c in range(n_emp)]
+    O = [occ_band(v) for v in range(n_occ)]
+    BEGIN, MID, LATE, FINISH, SENT = range(5)
+
+    def pass_on(v):
+        O[v][FINISH]()
+        share(v, core).start()
+
+    def shared(v):
+        share(v, 1 - core).wait_recv()
+
+    E[0][BEGIN]()
+    O[0][BEGIN]()
+    O[1][BEGIN]()
+    O[0][MID]()
+    E[0][MID]()
+    O[0][LATE]()
+    E[0][LATE]()
+    E[1][BEGIN]()
+    O[1][MID]()
+    O[2][BEGIN]()
+    O[1][LATE]()
+    O[3][BEGIN]()
+    pass_on(0)
+    O[2][MID]()
+    E[0][FINISH]()
+    shared(0)
+
+    steps = {
+        1: (O[2][LATE], O[3][MID], E[1][MID], lambda: pass_on(1), lambda: shared(1)),
+        2: (O[3][LATE], E[1][LATE], E[2][BEGIN], lambda: pass_on(2), lambda: shared(2)),
+        3: (lambda: pass_on(3), lambda: shared(3)),
+        4: (E[1][FINISH], E[2][MID], E[3][BEGIN]),
+        5: (E[2][LATE],),
+        6: (E[3][MID],),
+        7: (E[3][LATE],),
+        8: (E[2][FINISH],),
+        12: (E[3][FINISH],),
+    }
+    tile = TILE
+
+    def one_pair(n, carry):
+        c = n // n_occ
+        v = lax.rem(n, n_occ)
+        for step, actions in steps.items():
+
+            @pl.when(n == step)
+            def _(actions=actions):
+                for action in actions:
+                    action()
+
+        def one_tile(t, carry2):
+            high_rows = []
+            low_rows = []
+            for i in range(tile):
+                slab = t * tile + i
+                h, s = slab // 8, lax.rem(slab, 8)
+                real = []
+                imag = []
                 for q in range(3):
-                    lanes = pl.ds(pl.multiple_of((jt * tile + jj) * 384 + q * 128, 128), 128)
-                    vr = occ[0, v, :, lanes].astype(f32)
-                    vi = occ[1, v, :, lanes].astype(f32)
-                    cr = emp[0, 0, :, lanes].astype(f32)
-                    ci = emp[1, 0, :, lanes].astype(f32)
-                    res.append(vr * cr + vi * ci)
-                    ims.append(vr * ci - vi * cr)
-            rows = []
-            rows_lo = []
-            for jj in range(tile):
-                parts = res[3 * jj : 3 * jj + 3] + ims[3 * jj : 3 * jj + 3]
+                    vr = occ[v, h, s, 0, q].astype(f32)
+                    vi = occ[v, h, s, 1, q].astype(f32)
+                    cr = emp[c, h, s, 0, q].astype(f32)
+                    ci = emp[c, h, s, 1, q].astype(f32)
+                    real.append(vr * cr + vi * ci)
+                    imag.append(vr * ci - vi * cr)
+                parts = real + imag
                 high = [p.astype(bf16) for p in parts]
-                low = [(p - h.astype(f32)).astype(bf16) for p, h in zip(parts, high)]
-                rows.append(jnp.concatenate(high, axis=1))
-                rows_lo.append(jnp.concatenate(low, axis=1))
-            high = jnp.concatenate(rows, axis=0)
-            low = jnp.concatenate(rows_lo, axis=0)
+                low = [(p - h_.astype(f32)).astype(bf16) for p, h_ in zip(parts, high)]
+                high_rows.append(jnp.concatenate(high, axis=1))
+                low_rows.append(jnp.concatenate(low, axis=1))
+            high = jnp.concatenate(high_rows, axis=0)
+            low = jnp.concatenate(low_rows, axis=0)
             z = (
                 jnp.dot(high, t_hi[...], preferred_element_type=f32)
                 + jnp.dot(low, t_hi[...], preferred_element_type=f32)
                 + jnp.dot(high, t_lo[...], preferred_element_type=f32)
             )
             zh = z.astype(bf16)
-            where = pl.ds(pl.multiple_of(jt * (tile * GRID), 128), tile * GRID)
+            where = pl.ds(pl.multiple_of(t * (tile * ROWS), 16), tile * ROWS)
             z_hi[where, :] = zh
             z_lo[where, :] = (z - zh.astype(f32)).astype(bf16)
             return carry2
 
-        lax.fori_loop(0, GROUPS // tile, one_tile, 0)
+        lax.fori_loop(0, 16 // tile, one_tile, 0)
         both = (
             jnp.dot(a_hi[...], z_hi[...], preferred_element_type=f32)
             + jnp.dot(a_hi[...], z_lo[...], preferred_element_type=f32)
@@ -129,38 +322,53 @@
             qi = (cos * pi - s * (sin * pr)).T
             for at, q in ((0, qr), (1, qi)):
                 total = (q[:KZ] + q[KZ : 2 * KZ]) + (q[2 * KZ : 3 * KZ] + q[3 * KZ :])
-                out[at, v, 0, :, sign * HALF : (sign + 1) * HALF] = (total * w).astype(bf16)
+                out[at, v, c, :, sign * HALF : (sign + 1) * HALF] = (total * w).astype(bf16)
         return carry
 
-    lax.fori_loop(0, n_occ, one_band, 0)
-
-
-def compact(weight, occ_all, emp_all):
+    lax.fori_loop(0, n_occ * n_emp, one_pair, 0)
+    for v in range(n_occ):
+        O[v][SENT]()
+        share(v, core).wait_send()
+    for c in range(n_emp):
+        E[c][SENT]()
+
+
+TILE = 4
+
+
+def compact(weight, occupied, empty):
     (t_hi, t_lo), (a_hi, a_lo), tw, unused = tables()
-    n_occ, n_emp = occ_all.shape[1], emp_all.shape[1]
-    whole = lambda shape: pl.BlockSpec(shape, lambda c: (0,) * len(shape), pipeline_mode=pl.Buffered(1))
+    n_occ, n_emp = occupied.shape[1], empty.shape[1]
+    occ_in = occupied.reshape(2, n_occ, SLAB, GROUPS, 3, 128).transpose(1, 0, 4, 3, 2, 5)
+    occ_in = occ_in.reshape(n_occ, 2, 3, ROWS, 128)
+    emp_in = empty.reshape(2, n_emp, 2, SLAB, GROUPS, 3, 128).transpose(1, 2, 0, 5, 4, 3, 6)
+    emp_in = emp_in.reshape(n_emp, 2, 2, 3, ROWS, 128)
+    vmem = pl.BlockSpec(memory_space=pltpu.VMEM)
+    hbm = pl.BlockSpec(memory_space=pl.ANY)
+    dma = pltpu.SemaphoreType.DMA
     return pl.pallas_call(
         pair_kernel,
-        grid=(n_emp,),
         out_shape=jax.ShapeDtypeStruct((2, n_occ, n_emp, KZ, 2 * HALF), bf16),
-        in_specs=[
-            pl.BlockSpec(memory_space=pltpu.SMEM),
-            whole((2, n_occ, GRID, GRID * GRID)),
-            pl.BlockSpec((2, 1, GRID, GRID * GRID), lambda c: (0, c, 0, 0)),
-            whole((768, 256)),
-            whole((768, 256)),
-            whole((2 * HALF, GROUPS * GRID)),
-            whole((2 * HALF, GROUPS * GRID)),
-            whole((2, HALF, 128)),
-        ],
-        out_specs=pl.BlockSpec((2, n_occ, 1, KZ, 2 * HALF), lambda c: (0, 0, c, 0, 0)),
+        in_specs=[pl.BlockSpec(memory_space=pltpu.SMEM), hbm, hbm] + [vmem] * 5,
+        out_specs=vmem,
         scratch_shapes=[
+            pltpu.VMEM((n_occ, 2, 8, 2, 3, ROWS, 128), bf16),
+            pltpu.VMEM((n_emp, 2, 8, 2, 3, ROWS, 128), bf16),
             pltpu.VMEM((GROUPS * GRID, 256), bf16),
             pltpu.VMEM((GROUPS * GRID, 256), bf16),
+            dma((n_occ + n_emp,)),
+            dma((n_occ, KINDS)),
+            dma((n_occ, KINDS)),
+            dma((n_emp, KINDS)),
+            dma((n_emp, KINDS)),
+            dma((n_occ,)),
+            dma((n_occ,)),
         ],
-        compiler_params=pltpu.CompilerParams(vmem_limit_bytes=58 * 2**20),
+        compiler_params=pltpu.CompilerParams(
+            vmem_limit_bytes=60 * 2**20, collective_id=0, has_side_effects=True
+        ),
         name="pair_spectra",
-    )(weight, occ_all, emp_all, t_hi, t_lo, a_hi, a_lo, tw)
+    )(weight, occ_in, emp_in, t_hi, t_lo, a_hi, a_lo, tw)
 
 
 def select_kernel(column, kxy, kz, x, out):
@@ -206,16 +414,11 @@
 
 
 def body(occupied, empty, occ_energy, emp_energy, gvec):
-    emp_all = lax.all_gather(empty, "occ", axis=2, tiled=True)
-    occ_all = lax.all_gather(occupied, "emp", axis=2, tiled=True)
-    d = densities_of(occ_all, emp_all, occ_energy, emp_energy, gvec)
+    d = densities_of(occupied, empty, occ_energy, emp_energy, gvec)
     n_occ = lax.axis_size("occ")
     n_emp = lax.axis_size("emp")
     rows = d.shape[1]
-    r = d.reshape(n_occ, 1, 2, rows, BLOCK_PAD)
-    r = lax.all_to_all(r, "occ", split_axis=0, concat_axis=1, tiled=False) if False else lax.all_to_all(
-        d.reshape(n_occ, 2, rows, BLOCK_PAD), "occ", split_axis=0, concat_axis=0, tiled=True
-    )
+    r = lax.all_to_all(d.reshape(n_occ, 2, rows, BLOCK_PAD), "occ", split_axis=0, concat_axis=0, tiled=True)
     r = lax.all_gather(r, "emp", axis=0)
     c = lax.all_to_all(d, "emp", split_axis=0, concat_axis=0, tiled=True)
     c = lax.all_gather(c, "occ", axis=0)

time: 584 us -> 402 us (0.69)
  waiting for transfers between devices: 341 us -> 105 us
  Pallas kernels: 139 us -> 209 us
  local copies, waits for them, and re-layouts: 36.1 us -> 20.4 us
    all_gather x2 -> x0, waiting for transfers between devices: 235 us -> none  [the longest x1 147 us: body(): emp_all = lax.all_gather(empty, 'occ', axis=2, tiled=True)]
    pallas_call x1, Pallas kernels: 126 us -> 196 us  [compact(): pl.pallas_call(pair_kernel, out_shape=jax.ShapeDtypeStruct((2, n_occ, n_e...]
    all_gather x2 -> x0, local copies, waits for them, and re-layouts: 24.3 us -> none  [the longest x1 12.2 us: body(): occ_all = lax.all_gather(occupied, 'emp', axis=2, tiled=True)]
    reshape x0 -> x4, local copies, waits for them, and re-layouts: none -> 9.36 us  [the longest x1 4.25 us: compact(): empty.reshape(2, n_emp, 2, SLAB, GROUPS, 3, 128)]
  transfers between devices with their start and end apart: 4 -> 2, of which waited for: 4 -> 2; matrix products, arithmetic and copies ran while one was open for 3% -> 1% of each run, Pallas kernels for 0% -> 0%
where the time goes in v2:
time: 402 us; the launch traced here: 401 us
  Pallas kernels  209 us (52%)
  waiting for transfers between devices  105 us (26%)
  blocking collectives  28.9 us (7%)
  local copies, waits for them, and re-layouts  20.4 us (5%)
  matrix products  16.4 us (4%)
  between operations  13.5 us (3%)
  other arithmetic  8.29 us (2%)
    pallas_call x1, Pallas kernels, compact(): pl.pallas_call(pair_kernel, out_shape=jax.ShapeDtypeStruct((2, n_occ, n_e...  196 us
    all_gather x1, waiting for transfers between devices, body(): r = lax.all_gather(r, 'emp', axis=0)  66.1 us
    all_gather x1, waiting for transfers between devices, body(): c = lax.all_gather(c, 'occ', axis=0)  38.7 us
    all_to_all x1, blocking collectives, body(): lax.all_to_all(d.reshape(n_occ, 2, rows, BLOCK_PAD), 'occ', split_axis=0,...  14.8 us
    all_to_all x1, blocking collectives, body(): c = lax.all_to_all(d, 'emp', split_axis=0, concat_axis=0, tiled=True)  14.2 us
    pallas_call x1, Pallas kernels, select(): pl.pallas_call(select_kernel, grid=(blocks,), out_shape=jax.ShapeDtypeStr...  12.8 us
    dot_general x1, matrix products, body(): imag = lax.dot_general(left, turned, dims, preferred_element_type=f32)  8.21 us
    dot_general x1, matrix products, body(): real = lax.dot_general(left, c, dims, preferred_element_type=f32)  8.18 us
  transfers between devices with their start and end apart: 2, of which 2 were waited for; matrix products, arithmetic and copies ran while one was open for 1% of the time, Pallas kernels for 0%

profile of v2, /device:TPU:1, one launch (start us, length us, event | category | flops | bytes accessed | tf_op | source)
XLA Modules:
  0.0 401.4 jit_solution(5822882008292296915)
XLA Ops:
  6.5 0.9 reshape.23
  7.6 2.6 reshape.24
  10.2 1.1 copy.26
  11.3 1.1 copy.28.occ_in
  12.4 4.3 %reshape.26 = bf16[2,4,2,6,24,3,128]{6,5,4,1,3,2,0:T(4,128)(2,1)S(1)} reshape(bf16[2,4,12,9216]{3,1,2,0:T(4,128)(2,1)} %param.12) | data formatting | bytes 3538944 | tf_op jit(solution)/shard_map/reshape | solution.py:344
  16.6 2.1 copy.27
  18.8 1.4 copy.29.emp_in
  20.2 0.7 sqrt_multiply_fusion.weight
  21.0 196.1 %pair_spectra.1 = bf16[2,4,4,32,512]{4,3,2,1,0:T(8,128)(2,1)} custom-call(f32[4,4]{1,0:T(4,128)} %sqrt_multiply_fusion.weight, bf16[4,2,3,144,128]{4,3,2,1,0:T(8,128)(2,1)} %copy.28.occ_in, bf16[4,2,2,3,144,128]{5,4,3,2,1,0:T(8,128)(2,1)} %copy.29.emp_in, bf16[768,256]{1,0:T(8,128)(2,1)} %constant.36.clone.t_hi, bf16[768,256]{1,0:T(8,128)(2,1)} %constant.37.clone.t_lo, ...), custom_call_target="tpu_custom_call" | custom-call | tf_op jit(solution)/shard_map/pair_spectra/pallas_call | solution.py:349
  217.1 1.2 copy-done
  218.3 12.8 %sphere_select.1 = bf16[16,32,512]{2,1,0:T(8,128)(2,1)S(1)} custom-call(s32[512,1]{1,0:T(8,128)S(1)} %copy-done.1, s32[16,1,512]{2,1,0:T(1,128)S(1)} %broadcast_select_fusion.kxy, s32[16,1,512]{2,1,0:T(1,128)S(1)} %get-tuple-element.5.kz, bf16[1024,512]{1,0:T(8,128)(2,1)S(1)} %bitcast.48), custom_call_target="tpu_custom_call" | custom-call | tf_op jit(solution)/shard_map/sphere_select/pallas_call | solution.py:393
  231.1 14.2 %all_to_all.10 = bf16[16,32,512]{2,1,0:T(8,128)(2,1)} all-to-all(bf16[16,32,512]{2,1,0:T(8,128)(2,1)S(1)} %sphere_select.1), channel_id=1, replica_groups=mesh['occ'=8,'emp'=16] {'emp'}, dimensions={0} | all-to-all | bytes 1048576 | tf_op jit(solution)/shard_map/all_to_all | solution.py:423
  245.3 14.8 %all_to_all.11 = bf16[8,2,32,512]{3,2,1,0:T(8,128)(2,1)} all-to-all(bf16[8,2,32,512]{3,2,1,0:T(8,128)(2,1)S(1)} %bitcast.47), channel_id=1, replica_groups=mesh['occ'=8,'emp'=16] {'occ'}, dimensions={0} | all-to-all | bytes 1048576 | tf_op jit(solution)/shard_map/all_to_all | solution.py:421
  260.2 38.7 %all-gather.7.cloned.1.call-done = bf16[128,32,512]{2,1,0:T(8,128)(2,1)} async-done(((bf16[16,32,512]{2,1,0:T(8,128)(2,1)}), bf16[128,32,512]{2,1,0:T(8,128)(2,1)}) %all-gather.7.cloned.1.call-update) | async-done | bytes 4194320 | tf_op jit(solution)/shard_map/all_gather | solution.py:424
  298.9 2.7 copy.55
  301.5 2.3 slice_negate_fusion
  303.8 66.1 %all-gather.5.cloned.1.call-done = bf16[128,2,32,512]{3,2,1,0:T(8,128)(2,1)} async-done(((bf16[8,2,32,512]{3,2,1,0:T(8,128)(2,1)}), bf16[128,2,32,512]{3,2,1,0:T(8,128)(2,1)}) %all-gather.5.cloned.1.call-update) | async-done | bytes 8388624 | tf_op jit(solution)/shard_map/all_gather | solution.py:422
  369.9 8.2 %fusion.10 = f32[2,512,512]{2,1,0:T(8,128)S(1)} fusion(bf16[8,16,32,512]{3,2,1,0:T(8,128)(2,1)} %bitcast.54, bf16[16,8,2,32,512]{4,3,2,1,0:T(8,128)(2,1)} %bitcast.56), kind=kOutput, calls=%fused_computation.16 | convolution fusion | flops 4294967296 | bytes 14680064 | tf_op jit(solution)/shard_map/dot_general | solution.py:433
  378.1 0.2 slice_multiply_fusion.1
  378.4 1.6 stack_reshape.6
  380.0 8.2 %fusion.15 = f32[2,512,512]{2,1,0:T(8,128)S(1)} fusion(bf16[16,8,16,512]{3,2,1,0:T(8,128)(2,1)} %get-tuple-element.8, bf16[16,8,16,512]{3,2,1,0:T(8,128)(2,1)} %get-tuple-element.7, bf16[16,8,2,32,512]{4,3,2,1,0:T(8,128)(2,1)} %bitcast.57), kind=kOutput, calls=%fused_computation.17 | convolution fusion | flops 4303355904 | bytes 14680064 | tf_op jit(solution)/shard_map/dot_general | solution.py:434
  388.2 0.2 slice_multiply_fusion
  388.4 1.5 stack_reshape.7
  390.0 4.6 %pad_maximum_fusion = f32[2,1000,500]{2,1,0:T(8,128)} fusion(f32[1,1000,500]{2,1,0:T(8,128)} %stack_reshape.7, f32[1,1000,500]{2,1,0:T(8,128)} %stack_reshape.6), kind=kLoop, calls=%fused_computation.10 | loop fusion | flops 1000000 | bytes 8000000 | tf_op jit(solution)/shard_map/stack | solution.py:439
  (14 shorter events, 0.3 us)
Async XLA Ops:
  6.5 292.3 %all-gather.7.cloned.1.call-start = ((), (), s32[]{:S(2)}) async-start(), calls=%async_computation.3 | async-start | bytes 4718592 | tf_op jit(solution)/shard_map/all_gather | solution.py:424
  18.8 1.5 copy-start.2
  18.8 1.5 copy-start.3
  20.9 196.1 %copy-start.1 = (s32[512,1]{1,0:T(8,128)S(1)}, s32[512,1]{1,0:T(8,128)}, u32[]{:S(2)}) copy-start(s32[512,1]{1,0:T(8,128)} %constant.41.clone.column) | copy-start | bytes 6148
  217.1 1.2 copy-start
  245.3 124.7 %all-gather.5.cloned.1.call-start = ((), (), s32[]{:S(2)}) async-start(), calls=%async_computation.2 | async-start | bytes 8912896 | tf_op jit(solution)/shard_map/all_gather | solution.py:422
Sparse Core Ops, SparseCore 0:
  245.4 53.4 all-gather.6
  301.3 68.6 all-gather.4

commit v3 on v2

--- a/solution.py
+++ b/solution.py
@@ -76,7 +76,7 @@
 KINDS = 9
 
 
-def gather_steps(send, recv, shard, piece, hi, ring, device_of):
+def gather_steps(send, recv, shard, piece, hi, ring, device_of, landed=lambda i: None):
     own = hi * 4 + ring
     mate = (1 - hi) * 4 + ring
     right, left, far = lax.rem(ring + 1, 4), lax.rem(ring + 3, 4), lax.rem(ring + 2, 4)
@@ -128,6 +128,7 @@
 
     def begin():
         start(0, 1, 2)
+        landed(own)
 
     def mid():
         arrived(0)
@@ -136,15 +137,22 @@
         start(5)
         arrived(2)
         start(6)
+        landed(mate)
+        landed(from_left)
+        landed(from_right)
 
     def late():
         arrived(3)
         start(7)
         arrived(4)
         start(8)
+        landed(mate_left)
+        landed(mate_right)
 
     def finish():
         arrived(5, 6, 7, 8)
+        landed(across)
+        landed(mate_across)
 
     def sent():
         for kind in range(KINDS):
@@ -220,7 +228,6 @@
 
     E = [emp_band(c) for c in range(n_emp)]
     O = [occ_band(v) for v in range(n_occ)]
-    BEGIN, MID, LATE, FINISH, SENT = range(5)
 
     def pass_on(v):
         O[v][FINISH]()
@@ -413,30 +420,177 @@
     return select(gvec, x.reshape(rows * KZ, 2 * HALF))
 
 
+BEGIN, MID, LATE, FINISH, SENT = range(5)
+
+
+def chi_kernel(factor, d, out, rows, cols, local, r_send, r_recv, c_send, c_recv, g_send, g_recv, s_send, s_recv):
+    o = lax.axis_index("occ")
+    m = lax.axis_index("emp")
+    o_hi, o_ring = o // 4, lax.rem(o, 4)
+    chip, core = m // 2, lax.rem(m, 2)
+    c_hi, c_ring = chip // 4, lax.rem(chip, 4)
+
+    def copy(src, dst, send, recv, device):
+        return pltpu.make_async_remote_copy(
+            src_ref=src, dst_ref=dst, send_sem=send, recv_sem=recv, device_id=device, device_id_type=MESH
+        )
+
+    own_copies = [pltpu.make_async_copy(d.at[2 * o + b], rows.at[b, core, o, chip], local.at[b]) for b in range(2)]
+    own_copies.append(pltpu.make_async_copy(d.at[m], cols.at[core, o, chip], local.at[2]))
+    for own_copy in own_copies:
+        own_copy.start()
+
+    barrier = pltpu.get_barrier_semaphore()
+    for step in range(1, 8):
+        peer = {"occ": lax.rem(o + step, 8), "emp": m}
+        pl.semaphore_signal(barrier, inc=1, device_id=peer, device_id_type=MESH)
+    for step in range(1, 16):
+        peer = {"occ": o, "emp": lax.rem(m + step, 16)}
+        pl.semaphore_signal(barrier, inc=1, device_id=peer, device_id_type=MESH)
+    pl.semaphore_wait(barrier, 22)
+
+    def row_part(b, step):
+        to = lax.rem(o + step, 8)
+        return copy(
+            d.at[2 * to + b], rows.at[b, core, o, chip], r_send.at[b, step - 1], r_recv.at[b, step - 1],
+            {"occ": to, "emp": m},
+        )
+
+    def row_landing(b, step):
+        here = rows.at[b, core, lax.rem(o + 8 - step, 8), chip]
+        return copy(here, here, r_send.at[b, step - 1], r_recv.at[b, step - 1], {"occ": o, "emp": m})
+
+    def col_part(step):
+        to = lax.rem(m + step, 16)
+        return copy(
+            d.at[to], cols.at[core, o, chip], c_send.at[step - 1], c_recv.at[step - 1], {"occ": o, "emp": to}
+        )
+
+    def col_landing(step):
+        source = lax.rem(m + 16 - step, 16)
+        here = cols.at[lax.rem(source, 2), o, source // 2]
+        return copy(here, here, c_send.at[step - 1], c_recv.at[step - 1], {"occ": o, "emp": m})
+
+    row_steps = range(1, 8)
+    even, odd = range(2, 16, 2), range(1, 16, 2)
+    for step in row_steps:
+        row_part(0, step).start()
+    for step in even:
+        col_part(step).start()
+    for step in row_steps:
+        row_part(1, step).start()
+    for step in odd:
+        col_part(step).start()
+
+    sibling = {"occ": o, "emp": 2 * chip + 1 - core}
+
+    def share(b, mine, i):
+        here = rows.at[b, mine, :, i]
+        return copy(here, here, s_send.at[b, i], s_recv.at[b, i], sibling)
+
+    def row_band(b):
+        return gather_steps(
+            g_send.at[b], g_recv.at[b],
+            lambda i: rows.at[b, core, :, i],
+            lambda i, h: rows.at[b, core, pl.ds(4 * h, 4), i],
+            c_hi, c_ring,
+            lambda i: {"occ": o, "emp": 2 * i + core},
+            lambda i: share(b, core, i).start(),
+        )
+
+    def col_band(j):
+        k = core if j == 0 else 1 - core
+        return gather_steps(
+            g_send.at[2 + j], g_recv.at[2 + j],
+            lambda i: cols.at[k, i],
+            lambda i, h: cols.at[k, i, pl.ds(4 * h, 4)],
+            o_hi, o_ring,
+            lambda i: {"occ": i, "emp": m},
+        )
+
+    R = [row_band(b) for b in range(2)]
+    C = [col_band(j) for j in range(2)]
+    for own_copy in own_copies:
+        own_copy.wait()
+    for step in row_steps:
+        row_landing(0, step).wait_recv()
+    R[0][BEGIN]()
+    for step in even:
+        col_landing(step).wait_recv()
+    C[0][BEGIN]()
+    for step in row_steps:
+        row_landing(1, step).wait_recv()
+    R[1][BEGIN]()
+    for step in odd:
+        col_landing(step).wait_recv()
+    C[1][BEGIN]()
+    for part in (MID, LATE, FINISH):
+        for band in (R[0], C[0], R[1], C[1]):
+            band[part]()
+
+    depth = rows.shape[2] * rows.shape[3] * rows.shape[4]
+    half = rows.shape[4] // 2
+
+    def multiply(k, last):
+        right = cols[k].reshape(depth // (2 * half), 2 * half, BLOCK_PAD)
+        turned = jnp.concatenate([-right[:, half:], right[:, :half]], axis=1)
+        right = right.reshape(depth, BLOCK_PAD)
+        turned = turned.reshape(depth, BLOCK_PAD)
+        for b in range(2):
+            left = rows[b, k].reshape(depth, BLOCK_PAD)
+            for at, side in ((0, right), (1, turned)):
+                part = lax.dot_general(left, side, (((0,), (0,)), ((), ())), preferred_element_type=f32)
+                out[at, b] = (out[at, b] + part) * factor if last else part
+
+    multiply(core, False)
+    for b in range(2):
+        for i in range(8):
+            share(b, 1 - core, i).wait_recv()
+    multiply(1 - core, True)
+    for step in row_steps:
+        for b in range(2):
+            row_part(b, step).wait_send()
+    for step in range(1, 16):
+        col_part(step).wait_send()
+    for band in R + C:
+        band[SENT]()
+    for b in range(2):
+        for i in range(8):
+            share(b, core, i).wait_send()
+
+
 def body(occupied, empty, occ_energy, emp_energy, gvec):
     d = densities_of(occupied, empty, occ_energy, emp_energy, gvec)
+    rows = d.shape[1]
     n_occ = lax.axis_size("occ")
     n_emp = lax.axis_size("emp")
-    rows = d.shape[1]
-    r = lax.all_to_all(d.reshape(n_occ, 2, rows, BLOCK_PAD), "occ", split_axis=0, concat_axis=0, tiled=True)
-    r = lax.all_gather(r, "emp", axis=0)
-    c = lax.all_to_all(d, "emp", split_axis=0, concat_axis=0, tiled=True)
-    c = lax.all_gather(c, "occ", axis=0)
-    c = c.transpose(1, 0, 2, 3)
-    half = rows // 2
-    count = n_occ * n_emp * half
-    factor = -1.0 / math.sqrt(count)
-    cr, ci = c[:, :, :half], c[:, :, half:]
-    turned = jnp.concatenate([-ci, cr], axis=2)
-    dims = (((0, 1, 2), (0, 1, 2)), ((), ()))
-    left = r.transpose(0, 1, 3, 2, 4)
-    real = lax.dot_general(left, c, dims, preferred_element_type=f32)
-    imag = lax.dot_general(left, turned, dims, preferred_element_type=f32)
-
-    def trim(a):
-        return (a * factor)[:, :BLOCK, :BLOCK].reshape(2 * BLOCK, BLOCK)
-
-    return jnp.stack([trim(real), trim(imag)])
+    factor = -1.0 / math.sqrt(n_occ * n_emp * (rows // 2))
+    vmem = pl.BlockSpec(memory_space=pltpu.VMEM)
+    dma = pltpu.SemaphoreType.DMA
+    chi = pl.pallas_call(
+        functools.partial(chi_kernel, factor),
+        out_shape=jax.ShapeDtypeStruct((2, 2, BLOCK_PAD, BLOCK_PAD), f32),
+        in_specs=[pl.BlockSpec(memory_space=pl.ANY)],
+        out_specs=vmem,
+        scratch_shapes=[
+            pltpu.VMEM((2, 2, 8, 8, rows, BLOCK_PAD), bf16),
+            pltpu.VMEM((2, 8, 8, rows, BLOCK_PAD), bf16),
+            dma((3,)),
+            dma((2, 7)),
+            dma((2, 7)),
+            dma((15,)),
+            dma((15,)),
+            dma((4, KINDS)),
+            dma((4, KINDS)),
+            dma((2, 8)),
+            dma((2, 8)),
+        ],
+        compiler_params=pltpu.CompilerParams(
+            vmem_limit_bytes=56 * 2**20, collective_id=1, has_side_effects=True
+        ),
+        name="chi_blocks",
+    )(d)
+    return chi[:, :, :BLOCK, :BLOCK].reshape(2, 2 * BLOCK, BLOCK)
 
 
 def solution(mesh):

time: 402 us -> 301 us (0.75)
  waiting for transfers between devices: 105 us -> 0 us
  Pallas kernels: 209 us -> 275 us
  blocking collectives: 28.9 us -> 0 us
  matrix products: 16.4 us -> 0 us
  between operations: 13.5 us -> 0.11 us
  other arithmetic: 8.29 us -> 1.56 us
    all_gather x2 -> x0, waiting for transfers between devices: 105 us -> none  [the longest x1 66.1 us: body(): r = lax.all_gather(r, 'emp', axis=0)]
    pallas_call x0 -> x1, Pallas kernels: none -> 65.9 us  [body(): pl.pallas_call(functools.partial(chi_kernel, factor), out_shape=jax.Shape...]
    all_to_all x2 -> x0, blocking collectives: 28.9 us -> none  [the longest x1 14.8 us: body(): lax.all_to_all(d.reshape(n_occ, 2, rows, BLOCK_PAD), 'occ', split_axis=0,...]
    dot_general x2 -> x0, matrix products: 16.4 us -> none  [the longest x1 8.21 us: body(): imag = lax.dot_general(left, turned, dims, preferred_element_type=f32)]
    another operation x1 -> x0, other arithmetic: 4.61 us -> none  [body(): return jnp.stack([trim(real), trim(imag)])]
    slice x0 -> x1, local copies, waits for them, and re-layouts: none -> 4.56 us  [body(): return chi[:, :, :BLOCK, :BLOCK].reshape(2, 2 * BLOCK, BLOCK)]
  transfers between devices with their start and end apart: 2 -> 0, of which waited for: 2 -> 0; matrix products, arithmetic and copies ran while one was open for 1% -> 0% of each run, Pallas kernels for 0% -> 0%
where the time goes in v3:
time: 301 us; the launch traced here: 300 us
  Pallas kernels  275 us (91%)
  local copies, waits for them, and re-layouts  23.7 us (8%)
    pallas_call x1, Pallas kernels, compact(): pl.pallas_call(pair_kernel, out_shape=jax.ShapeDtypeStruct((2, n_occ, n_e...  196 us
    pallas_call x1, Pallas kernels, body(): pl.pallas_call(functools.partial(chi_kernel, factor), out_shape=jax.Shape...  65.9 us
    pallas_call x1, Pallas kernels, select(): pl.pallas_call(select_kernel, grid=(blocks,), out_shape=jax.ShapeDtypeStr...  13 us

profile of v3, /device:TPU:1, one launch (start us, length us, event | category | flops | bytes accessed | tf_op | source)
XLA Modules:
  0.0 300.4 jit_solution(13819998855618902699)
XLA Ops:
  0.0 1.3 sqrt_multiply_fusion.weight
  1.3 0.9 reshape.23
  2.2 0.2 multiply_subtract_fusion
  2.5 2.6 reshape.24
  5.1 1.1 copy.14
  6.1 1.1 copy.16.occ_in
  7.2 4.3 %reshape.26 = bf16[2,4,2,6,24,3,128]{6,5,4,1,3,2,0:T(4,128)(2,1)S(1)} reshape(bf16[2,4,12,9216]{3,1,2,0:T(4,128)(2,1)} %param.12) | data formatting | bytes 3538944 | tf_op jit(solution)/shard_map/reshape | solution.py:351
  11.5 2.1 copy.15
  13.6 1.4 copy.17.emp_in
  15.0 0.0 copy-start.2
  15.0 196.0 %pair_spectra.1 = bf16[2,4,4,32,512]{4,3,2,1,0:T(8,128)(2,1)} custom-call(f32[4,4]{1,0:T(4,128)} %sqrt_multiply_fusion.weight, bf16[4,2,3,144,128]{4,3,2,1,0:T(8,128)(2,1)} %copy.16.occ_in, bf16[4,2,2,3,144,128]{5,4,3,2,1,0:T(8,128)(2,1)} %copy.17.emp_in, bf16[768,256]{1,0:T(8,128)(2,1)} %constant.34.clone.t_hi, bf16[768,256]{1,0:T(8,128)(2,1)} %constant.35.clone.t_lo, ...), custom_call_target="tpu_custom_call" | custom-call | tf_op jit(solution)/shard_map/pair_spectra/pallas_call | solution.py:356
  211.1 0.0 copy-done.2
  211.1 0.0 copy-start
  211.1 1.2 copy-done
  212.3 13.0 %sphere_select.1.d = bf16[16,32,512]{2,1,0:T(8,128)(2,1)S(1)} custom-call(s32[512,1]{1,0:T(8,128)S(1)} %copy-done.2, s32[16,1,512]{2,1,0:T(1,128)S(1)} %broadcast_select_fusion.kxy, s32[16,1,512]{2,1,0:T(1,128)S(1)} %get-tuple-element.5.kz, bf16[1024,512]{1,0:T(8,128)(2,1)S(1)} %bitcast.9), custom_call_target="tpu_custom_call" | custom-call | tf_op jit(solution)/shard_map/sphere_select/pallas_call | solution.py:400
  225.3 0.0 copy-start.1
  225.3 0.8 copy-done.1
  226.1 65.9 %chi_blocks.1 = f32[2,2,512,512]{3,2,1,0:T(8,128)} custom-call(bf16[16,32,512]{2,1,0:T(8,128)(2,1)} %copy-done.1), custom_call_target="tpu_custom_call" | custom-call | tf_op jit(solution)/shard_map/chi_blocks/pallas_call | solution.py:570
  292.0 4.6 %slice.3 = f32[2,2,500,500]{3,2,1,0:T(8,128)} slice(f32[2,2,512,512]{3,2,1,0:T(8,128)} %chi_blocks.1), slice={[0:2], [0:2], [0:500], [0:500]} | slice | bytes 8000000 | tf_op jit(solution)/shard_map/slice | solution.py:593
  296.6 3.8 %reshape.29 = f32[2,1000,500]{2,1,0:T(8,128)} reshape(f32[2,2,500,500]{3,2,1,0:T(8,128)} %slice.3) | data formatting | bytes 8000000 | tf_op jit(solution)/shard_map/reshape | solution.py:593
  (2 shorter events, 0.0 us)
Async XLA Ops:
  15.0 196.0 %copy-start.2 = (s32[512,1]{1,0:T(8,128)S(1)}, s32[512,1]{1,0:T(8,128)}, u32[]{:S(2)}) copy-start(s32[512,1]{1,0:T(8,128)} %constant.39.clone.column) | copy-start | bytes 6148
  211.1 1.2 copy-start
  225.3 0.8 copy-start.1

commit v4 on v3

--- a/solution.py
+++ b/solution.py
@@ -20,6 +20,8 @@
 ROWS = GROUPS * SLAB
 HALF = 256
 KZ = 32
+CHUNK_Y = ((0, 1), (2, 1), (2, 3))
+RING_FIRST = ()
 BLOCK = 500
 BLOCK_PAD = 512
 
@@ -47,14 +49,17 @@
     disc = half_disc()
     kx, ky = disc[:, 0], disc[:, 1]
     freq = (np.arange(KB) + REACH) % KB - REACH
-    angle = theta * (np.outer(np.arange(GRID), freq) % GRID)
-    first = np.zeros((2, 4, GRID, 2, 4, KZ))
-    for y in range(4):
-        first[0, y, :, 0, y, :KB] = np.cos(angle)
-        first[0, y, :, 1, y, :KB] = -np.sin(angle)
-        first[1, y, :, 0, y, :KB] = np.sin(angle)
-        first[1, y, :, 1, y, :KB] = np.cos(angle)
-    first = first.reshape(768, 256)
+    first = np.zeros((3, 2, 128, 2, 2, KZ))
+    for q in range(3):
+        for lane in range(128):
+            y, z = divmod(q * 128 + lane, GRID)
+            slot = CHUNK_Y[q].index(y)
+            angle = theta * (z * freq % GRID)
+            first[q, 0, lane, slot, 0, :KB] = np.cos(angle)
+            first[q, 0, lane, slot, 1, :KB] = -np.sin(angle)
+            first[q, 1, lane, slot, 0, :KB] = np.sin(angle)
+            first[q, 1, lane, slot, 1, :KB] = np.cos(angle)
+    first = first.reshape(768, 128)
     half, slab, j, x = [a.reshape(-1) for a in np.meshgrid(*map(np.arange, (2, 8, GROUPS, SLAB)), indexing="ij")]
     x = 2 * SLAB * slab + SLAB * half + x
     angle = theta * ((np.outer(kx, x) + 4 * np.outer(ky, j)) % GRID)
@@ -62,21 +67,25 @@
     second[0, : len(disc)] = np.cos(angle)
     second[1, : len(disc)] = np.sin(angle)
     second = second.reshape(2 * HALF, GROUPS * GRID)
-    angle = theta * ((ky[:, None] * np.repeat(np.arange(4), KZ)[None, :]) % GRID)
-    twiddle = np.zeros((2, HALF, 4 * KZ), np.float32)
+    angle = theta * ((ky[:, None] * np.repeat(np.arange(4), 2 * KZ)[None, :]) % GRID)
+    turn = np.tile(np.repeat([1.0, -1.0], KZ), 4)
+    twiddle = np.zeros((2, HALF, 8 * KZ), np.float32)
     twiddle[0, : len(disc)] = np.cos(angle)
-    twiddle[1, : len(disc)] = np.sin(angle)
+    twiddle[1, : len(disc)] = np.sin(angle) * turn
     column = np.full((2, HALF), -1, np.int32)
     column[0, : len(disc)] = (kx % KB) * KB + ky % KB
     column[1, 1 : len(disc)] = ((-kx) % KB)[1:] * KB + ((-ky) % KB)[1:]
-    return split(first), split(second), twiddle, column.reshape(2 * HALF, 1)
+    first_hi, first_lo = split(first)
+    first = np.concatenate([first_hi, first_lo], axis=1)
+    second = np.concatenate(split(second), axis=0)
+    return first, second, twiddle, column.reshape(2 * HALF, 1)
 
 
 MESH = pl.DeviceIdType.MESH
 KINDS = 9
 
 
-def gather_steps(send, recv, shard, piece, hi, ring, device_of, landed=lambda i: None):
+def gather_steps(send, recv, shard, piece, hi, ring, device_of, landed=lambda i: None, ring_first=False):
     own = hi * 4 + ring
     mate = (1 - hi) * 4 + ring
     right, left, far = lax.rem(ring + 1, 4), lax.rem(ring + 3, 4), lax.rem(ring + 2, 4)
@@ -95,17 +104,19 @@
     from_left, from_right, across = hi * 4 + left, hi * 4 + right, hi * 4 + far
     mate_left, mate_right, mate_across = (1 - hi) * 4 + left, (1 - hi) * 4 + right, (1 - hi) * 4 + far
 
+    if ring_first:
+        relays = [(3, shard(from_left), mate), (4, shard(from_right), mate)]
+        relays += [(5, piece(from_left, 0), to_right), (6, piece(from_right, 1), to_left)]
+        relays += [(7, piece(across, 0), mate), (8, piece(across, 1), mate)]
+    else:
+        relays = [(3, shard(mate), to_right), (4, shard(mate), to_left)]
+        relays += [(5, piece(from_left, 0), to_right), (6, piece(from_right, 1), to_left)]
+        relays += [(7, piece(mate_left, 0), to_right), (8, piece(mate_right, 1), to_left)]
     sends = [
         (0, shard(own), mate),
         (1, shard(own), to_right),
         (2, shard(own), to_left),
-        (3, shard(mate), to_right),
-        (4, shard(mate), to_left),
-        (5, piece(from_left, 0), to_right),
-        (6, piece(from_right, 1), to_left),
-        (7, piece(mate_left, 0), to_right),
-        (8, piece(mate_right, 1), to_left),
-    ]
+    ] + relays
     landings = [
         shard(mate),
         shard(from_left),
@@ -131,17 +142,29 @@
         landed(own)
 
     def mid():
-        arrived(0)
-        start(3, 4)
-        arrived(1)
-        start(5)
-        arrived(2)
-        start(6)
+        if ring_first:
+            arrived(1)
+            start(5, 3)
+            arrived(2)
+            start(6, 4)
+        else:
+            arrived(0)
+            start(3, 4)
+            arrived(1)
+            start(5)
+            arrived(2)
+            start(6)
         landed(mate)
         landed(from_left)
         landed(from_right)
 
     def late():
+        if ring_first:
+            arrived(5)
+            start(7)
+            arrived(6)
+            start(8)
+            return
         arrived(3)
         start(7)
         arrived(4)
@@ -150,6 +173,9 @@
         landed(mate_right)
 
     def finish():
+        if ring_first:
+            arrived(0, 3, 4, 7, 8)
+            return
         arrived(5, 6, 7, 8)
         landed(across)
         landed(mate_across)
@@ -162,8 +188,8 @@
 
 
 def pair_kernel(
-    weight, occ_in, emp_in, t_hi, t_lo, a_hi, a_lo, tw, out,
-    occ, emp, z_hi, z_lo, local, o_send, o_recv, e_send, e_recv, s_send, s_recv,
+    weight, occ_in, emp_in, first, second, tw, out,
+    occ, emp, z_hi, z_lo, high_0, low_0, high_1, low_1, local, o_send, o_recv, e_send, e_recv, s_send, s_recv,
 ):
     n_occ, n_emp = occ.shape[0], emp.shape[0]
     o = lax.axis_index("occ")
@@ -179,6 +205,7 @@
             lambda i, h: emp.at[c, h, i],
             o_hi, o_ring,
             lambda i: {"occ": i, "emp": m},
+            ring_first=c in RING_FIRST,
         )
 
     def occ_band(v):
@@ -236,103 +263,145 @@
     def shared(v):
         share(v, 1 - core).wait_recv()
 
-    E[0][BEGIN]()
-    O[0][BEGIN]()
-    O[1][BEGIN]()
-    O[0][MID]()
-    E[0][MID]()
-    O[0][LATE]()
-    E[0][LATE]()
-    E[1][BEGIN]()
-    O[1][MID]()
-    O[2][BEGIN]()
-    O[1][LATE]()
-    O[3][BEGIN]()
-    pass_on(0)
-    O[2][MID]()
-    E[0][FINISH]()
-    shared(0)
+    for action in (
+        E[0][BEGIN],
+        O[0][BEGIN],
+        O[1][BEGIN],
+        O[2][BEGIN],
+        O[3][BEGIN],
+        E[1][BEGIN],
+        E[0][MID],
+        O[0][MID],
+        O[1][MID],
+        O[0][LATE],
+        E[0][LATE],
+        E[2][BEGIN],
+        O[1][LATE],
+        O[2][MID],
+        lambda: pass_on(0),
+        O[3][MID],
+        O[2][LATE],
+        E[0][FINISH],
+        E[3][BEGIN],
+        lambda: shared(0),
+    ):
+        action()
 
     steps = {
-        1: (O[2][LATE], O[3][MID], E[1][MID], lambda: pass_on(1), lambda: shared(1)),
-        2: (O[3][LATE], E[1][LATE], E[2][BEGIN], lambda: pass_on(2), lambda: shared(2)),
-        3: (lambda: pass_on(3), lambda: shared(3)),
-        4: (E[1][FINISH], E[2][MID], E[3][BEGIN]),
-        5: (E[2][LATE],),
-        6: (E[3][MID],),
-        7: (E[3][LATE],),
-        8: (E[2][FINISH],),
-        12: (E[3][FINISH],),
+        1: (lambda: pass_on(1), E[1][MID], O[3][LATE],),
+        4: (lambda: shared(1),),
+        5: (E[1][LATE],),
+        6: (lambda: pass_on(2),),
+        7: (E[2][MID],),
+        8: (lambda: shared(2),),
+        11: (E[2][LATE],),
+        12: (E[1][FINISH],),
+        13: (E[3][MID],),
+        14: (lambda: pass_on(3),),
+        17: (E[3][LATE],),
+        19: (lambda: shared(3),),
+        32: (E[2][FINISH],),
+        48: (E[3][FINISH],),
     }
-    tile = TILE
+
+    pairs = n_occ * n_emp
+    highs, lows = (high_0, high_1), (low_0, low_1)
+
+    def pair_at(n):
+        late, extra = n // 8, n // 6
+        early = 1 - late
+        first_six = early * (1 - lax.rem(extra, 2))
+        pair_of_last = early - first_six
+        c = first_six * (n // 3) + pair_of_last * (n - 6) + late * (n // 4)
+        v = first_six * lax.rem(n, 3) + pair_of_last * 3 + late * lax.rem(n, 4)
+        return v, c
+
+    def products(n, t):
+        v, c = pair_at(n)
+        high_to, low_to = highs[t % 2], lows[t % 2]
+        for i in range(TILE):
+            slab = t * TILE + i
+            h, s = slab // 8, slab % 8
+            rows = slice(i * ROWS, (i + 1) * ROWS)
+            for q in range(3):
+                vr = occ[v, h, s, 0, q].astype(f32)
+                vi = occ[v, h, s, 1, q].astype(f32)
+                cr = emp[c, h, s, 0, q].astype(f32)
+                ci = emp[c, h, s, 1, q].astype(f32)
+                for at, p in ((0, vr * cr + vi * ci), (1, vr * ci - vi * cr)):
+                    lanes = slice((2 * q + at) * 128, (2 * q + at + 1) * 128)
+                    high = p.astype(bf16)
+                    high_to[rows, lanes] = high
+                    low_to[rows, lanes] = (p - high.astype(f32)).astype(bf16)
+
+    def transform_z(t):
+        high, low = highs[t % 2], lows[t % 2]
+        parts = []
+        for q in range(3):
+            table = first[q * 256 : (q + 1) * 256, :]
+            chunk = slice(q * 256, (q + 1) * 256)
+            both = jnp.dot(high[:, chunk], table, preferred_element_type=f32)
+            more = jnp.dot(low[:, chunk], table[:, :128], preferred_element_type=f32)
+            parts.append(both[:, :128] + (both[:, 128:] + more))
+        upper = lax.broadcasted_iota(jnp.int32, parts[1].shape, 1) >= 64
+        zero = jnp.zeros_like(parts[1])
+        for at, z in (
+            (0, parts[0] + jnp.where(upper, parts[1], zero)),
+            (1, parts[2] + jnp.where(upper, zero, parts[1])),
+        ):
+            where = (slice(t * TILE * ROWS, (t + 1) * TILE * ROWS), slice(at * 128, (at + 1) * 128))
+            high_z = z.astype(bf16)
+            z_hi[where] = high_z
+            z_lo[where] = (z - high_z.astype(f32)).astype(bf16)
+
+    def swap(a):
+        real = lax.rem(lax.broadcasted_iota(jnp.int32, a.shape, 1) // KZ, 2) == 0
+        return jnp.where(real, pltpu.roll(a, a.shape[1] - KZ, 1), pltpu.roll(a, KZ, 1))
+
+    def transform_xy(n):
+        v, c = pair_at(n)
+        big = jnp.dot(second[...], z_hi[...], preferred_element_type=f32)
+        small = jnp.dot(second[: 2 * HALF, :], z_lo[...], preferred_element_type=f32)
+        both = big[: 2 * HALF] + (big[2 * HALF :] + small)
+        u = both[:HALF]
+        real = lax.rem(lax.broadcasted_iota(jnp.int32, u.shape, 1) // KZ, 2) == 0
+        w = swap(both[HALF:])
+        w = jnp.where(real, w, -w)
+        cos, sin = tw[0], tw[1]
+        scale = weight[v, c]
+        for sign in range(2):
+            g = u + w if sign == 0 else u - w
+            turned = sin * swap(g)
+            full = (cos * g + turned if sign == 0 else cos * g - turned).T
+            total = (full[: 2 * KZ] + full[2 * KZ : 4 * KZ]) + (full[4 * KZ : 6 * KZ] + full[6 * KZ :])
+            total = (total * scale).astype(bf16).reshape(2, KZ, HALF)
+            out[:, v, c, :, sign * HALF : (sign + 1) * HALF] = total
+
+    products(0, 0)
+
+    tiles = 16 // TILE
+
+    def serve(n, t):
+        for step, actions in steps.items():
+            if step % tiles == t:
+
+                @pl.when(n == step // tiles)
+                def _(actions=actions):
+                    for action in actions:
+                        action()
 
     def one_pair(n, carry):
-        c = n // n_occ
-        v = lax.rem(n, n_occ)
-        for step, actions in steps.items():
-
-            @pl.when(n == step)
-            def _(actions=actions):
-                for action in actions:
-                    action()
-
-        def one_tile(t, carry2):
-            high_rows = []
-            low_rows = []
-            for i in range(tile):
-                slab = t * tile + i
-                h, s = slab // 8, lax.rem(slab, 8)
-                real = []
-                imag = []
-                for q in range(3):
-                    vr = occ[v, h, s, 0, q].astype(f32)
-                    vi = occ[v, h, s, 1, q].astype(f32)
-                    cr = emp[c, h, s, 0, q].astype(f32)
-                    ci = emp[c, h, s, 1, q].astype(f32)
-                    real.append(vr * cr + vi * ci)
-                    imag.append(vr * ci - vi * cr)
-                parts = real + imag
-                high = [p.astype(bf16) for p in parts]
-                low = [(p - h_.astype(f32)).astype(bf16) for p, h_ in zip(parts, high)]
-                high_rows.append(jnp.concatenate(high, axis=1))
-                low_rows.append(jnp.concatenate(low, axis=1))
-            high = jnp.concatenate(high_rows, axis=0)
-            low = jnp.concatenate(low_rows, axis=0)
-            z = (
-                jnp.dot(high, t_hi[...], preferred_element_type=f32)
-                + jnp.dot(low, t_hi[...], preferred_element_type=f32)
-                + jnp.dot(high, t_lo[...], preferred_element_type=f32)
-            )
-            zh = z.astype(bf16)
-            where = pl.ds(pl.multiple_of(t * (tile * ROWS), 16), tile * ROWS)
-            z_hi[where, :] = zh
-            z_lo[where, :] = (z - zh.astype(f32)).astype(bf16)
-            return carry2
-
-        lax.fori_loop(0, 16 // tile, one_tile, 0)
-        both = (
-            jnp.dot(a_hi[...], z_hi[...], preferred_element_type=f32)
-            + jnp.dot(a_hi[...], z_lo[...], preferred_element_type=f32)
-            + jnp.dot(a_lo[...], z_hi[...], preferred_element_type=f32)
-        )
-        ur = both[:HALF, :128]
-        ui = both[:HALF, 128:]
-        wr = both[HALF:, :128]
-        wi = both[HALF:, 128:]
-        cos, sin = tw[0], tw[1]
-        w = weight[v, c]
-        for sign in range(2):
-            s = 1.0 - 2.0 * sign
-            pr = ur + s * wi
-            pi = ui - s * wr
-            qr = (cos * pr + s * (sin * pi)).T
-            qi = (cos * pi - s * (sin * pr)).T
-            for at, q in ((0, qr), (1, qi)):
-                total = (q[:KZ] + q[KZ : 2 * KZ]) + (q[2 * KZ : 3 * KZ] + q[3 * KZ :])
-                out[at, v, c, :, sign * HALF : (sign + 1) * HALF] = (total * w).astype(bf16)
+        for t in range(tiles):
+            transform_z(t)
+            if t + 1 < tiles:
+                serve(n, t + 1)
+                products(n, t + 1)
+        serve(n + 1, 0)
+        transform_xy(n)
+        products(jnp.minimum(n + 1, pairs - 1), 0)
         return carry
 
-    lax.fori_loop(0, n_occ * n_emp, one_pair, 0)
+    lax.fori_loop(0, pairs, one_pair, 0)
     for v in range(n_occ):
         O[v][SENT]()
         share(v, core).wait_send()
@@ -344,7 +413,7 @@
 
 
 def compact(weight, occupied, empty):
-    (t_hi, t_lo), (a_hi, a_lo), tw, unused = tables()
+    first, second, tw, unused = tables()
     n_occ, n_emp = occupied.shape[1], empty.shape[1]
     occ_in = occupied.reshape(2, n_occ, SLAB, GROUPS, 3, 128).transpose(1, 0, 4, 3, 2, 5)
     occ_in = occ_in.reshape(n_occ, 2, 3, ROWS, 128)
@@ -356,13 +425,17 @@
     return pl.pallas_call(
         pair_kernel,
         out_shape=jax.ShapeDtypeStruct((2, n_occ, n_emp, KZ, 2 * HALF), bf16),
-        in_specs=[pl.BlockSpec(memory_space=pltpu.SMEM), hbm, hbm] + [vmem] * 5,
+        in_specs=[pl.BlockSpec(memory_space=pltpu.SMEM), hbm, hbm] + [vmem] * 3,
         out_specs=vmem,
         scratch_shapes=[
             pltpu.VMEM((n_occ, 2, 8, 2, 3, ROWS, 128), bf16),
             pltpu.VMEM((n_emp, 2, 8, 2, 3, ROWS, 128), bf16),
             pltpu.VMEM((GROUPS * GRID, 256), bf16),
             pltpu.VMEM((GROUPS * GRID, 256), bf16),
+            pltpu.VMEM((TILE * ROWS, 768), bf16),
+            pltpu.VMEM((TILE * ROWS, 768), bf16),
+            pltpu.VMEM((TILE * ROWS, 768), bf16),
+            pltpu.VMEM((TILE * ROWS, 768), bf16),
             dma((n_occ + n_emp,)),
             dma((n_occ, KINDS)),
             dma((n_occ, KINDS)),
@@ -375,7 +448,7 @@
             vmem_limit_bytes=60 * 2**20, collective_id=0, has_side_effects=True
         ),
         name="pair_spectra",
-    )(weight, occ_in, emp_in, t_hi, t_lo, a_hi, a_lo, tw)
+    )(weight, occ_in, emp_in, first, second, tw)
 
 
 def select_kernel(column, kxy, kz, x, out):

time: 301 us -> 306 us (1.017)
  Pallas kernels: 275 us -> 280 us
    pallas_call x1, Pallas kernels: 65.9 us -> 69 us  [body(): pl.pallas_call(functools.partial(chi_kernel, factor), out_shape=jax.Shape...]
where the time goes in v4:
time: 306 us; the launch traced here: 305 us
  Pallas kernels  280 us (92%)
  local copies, waits for them, and re-layouts  23.7 us (8%)
    pallas_call x1, Pallas kernels, compact(): pl.pallas_call(pair_kernel, out_shape=jax.ShapeDtypeStruct((2, n_occ, n_e...  198 us
    pallas_call x1, Pallas kernels, body(): pl.pallas_call(functools.partial(chi_kernel, factor), out_shape=jax.Shape...  69 us
    pallas_call x1, Pallas kernels, select(): pl.pallas_call(select_kernel, grid=(blocks,), out_shape=jax.ShapeDtypeStr...  12.8 us

profile of v4, /device:TPU:1, one launch (start us, length us, event | category | flops | bytes accessed | tf_op | source)
XLA Modules:
  0.0 305.2 jit_solution(7223822598116177133)
XLA Ops:
  0.0 1.3 sqrt_multiply_fusion.weight
  1.3 0.9 reshape.23
  2.2 0.2 multiply_subtract_fusion
  2.5 2.6 reshape.24
  5.1 1.1 copy.12
  6.1 1.1 copy.14.occ_in
  7.2 4.3 %reshape.26 = bf16[2,4,2,6,24,3,128]{6,5,4,1,3,2,0:T(4,128)(2,1)S(1)} reshape(bf16[2,4,12,9216]{3,1,2,0:T(4,128)(2,1)} %param.10) | data formatting | bytes 3538944 | tf_op jit(solution)/shard_map/reshape | solution.py:420
  11.5 2.1 copy.13
  13.6 1.4 copy.15.emp_in
  15.0 0.0 copy-start.2
  15.0 198.0 %pair_spectra.1 = bf16[2,4,4,32,512]{4,3,2,1,0:T(8,128)(2,1)} custom-call(f32[4,4]{1,0:T(4,128)} %sqrt_multiply_fusion.weight, bf16[4,2,3,144,128]{4,3,2,1,0:T(8,128)(2,1)} %copy.14.occ_in, bf16[4,2,2,3,144,128]{5,4,3,2,1,0:T(8,128)(2,1)} %copy.15.emp_in, bf16[768,256]{1,0:T(8,128)(2,1)} %constant.30.clone.first, bf16[1024,2304]{1,0:T(8,128)(2,1)} %constant.31.clone.second, ...), custom_call_target="tpu_custom_call" | custom-call | tf_op jit(solution)/shard_map/pair_spectra/pallas_call | solution.py:425
  213.0 0.0 copy-done.2
  213.1 0.0 copy-start
  213.1 1.2 copy-done
  214.3 12.8 %sphere_select.1.d = bf16[16,32,512]{2,1,0:T(8,128)(2,1)S(1)} custom-call(s32[512,1]{1,0:T(8,128)S(1)} %copy-done.2, s32[16,1,512]{2,1,0:T(1,128)S(1)} %broadcast_select_fusion.kxy, s32[16,1,512]{2,1,0:T(1,128)S(1)} %get-tuple-element.5.kz, bf16[1024,512]{1,0:T(8,128)(2,1)S(1)} %bitcast.9), custom_call_target="tpu_custom_call" | custom-call | tf_op jit(solution)/shard_map/sphere_select/pallas_call | solution.py:473
  227.1 0.0 copy-start.1
  227.1 0.8 copy-done.1
  227.9 69.0 %chi_blocks.1 = f32[2,2,512,512]{3,2,1,0:T(8,128)} custom-call(bf16[16,32,512]{2,1,0:T(8,128)(2,1)} %copy-done.1), custom_call_target="tpu_custom_call" | custom-call | tf_op jit(solution)/shard_map/chi_blocks/pallas_call | solution.py:643
  296.9 4.6 %slice.3 = f32[2,2,500,500]{3,2,1,0:T(8,128)} slice(f32[2,2,512,512]{3,2,1,0:T(8,128)} %chi_blocks.1), slice={[0:2], [0:2], [0:500], [0:500]} | slice | bytes 8000000 | tf_op jit(solution)/shard_map/slice | solution.py:666
  301.5 3.8 %reshape.29 = f32[2,1000,500]{2,1,0:T(8,128)} reshape(f32[2,2,500,500]{3,2,1,0:T(8,128)} %slice.3) | data formatting | bytes 8000000 | tf_op jit(solution)/shard_map/reshape | solution.py:666
  (2 shorter events, 0.0 us)
Async XLA Ops:
  15.0 198.0 %copy-start.2 = (s32[512,1]{1,0:T(8,128)S(1)}, s32[512,1]{1,0:T(8,128)}, u32[]{:S(2)}) copy-start(s32[512,1]{1,0:T(8,128)} %constant.33.clone.column) | copy-start | bytes 6148
  213.1 1.2 copy-start
  227.1 0.8 copy-start.1

commit v5 on v4

--- a/solution.py
+++ b/solution.py
@@ -267,39 +267,36 @@
         E[0][BEGIN],
         O[0][BEGIN],
         O[1][BEGIN],
+        O[0][MID],
+        E[0][MID],
+        O[0][LATE],
         O[2][BEGIN],
+        lambda: pass_on(0),
+        E[0][LATE],
+        E[1][BEGIN],
+        O[1][MID],
+        O[1][LATE],
         O[3][BEGIN],
-        E[1][BEGIN],
-        E[0][MID],
-        O[0][MID],
-        O[1][MID],
-        O[0][LATE],
-        E[0][LATE],
-        E[2][BEGIN],
-        O[1][LATE],
-        O[2][MID],
-        lambda: pass_on(0),
-        O[3][MID],
-        O[2][LATE],
         E[0][FINISH],
-        E[3][BEGIN],
         lambda: shared(0),
     ):
         action()
 
     steps = {
-        1: (lambda: pass_on(1), E[1][MID], O[3][LATE],),
-        4: (lambda: shared(1),),
-        5: (E[1][LATE],),
-        6: (lambda: pass_on(2),),
-        7: (E[2][MID],),
-        8: (lambda: shared(2),),
-        11: (E[2][LATE],),
-        12: (E[1][FINISH],),
-        13: (E[3][MID],),
-        14: (lambda: pass_on(3),),
-        17: (E[3][LATE],),
-        19: (lambda: shared(3),),
+        2: (lambda: pass_on(1),),
+        3: (E[1][MID], E[2][BEGIN],),
+        4: (lambda: shared(1), O[2][MID],),
+        6: (E[1][LATE],),
+        7: (O[2][LATE],),
+        8: (lambda: pass_on(2), lambda: shared(2),),
+        10: (O[3][MID],),
+        12: (E[1][FINISH], E[2][MID], E[3][BEGIN],),
+        13: (O[3][LATE],),
+        15: (lambda: pass_on(3),),
+        17: (E[2][LATE],),
+        18: (lambda: shared(3),),
+        23: (E[3][MID],),
+        28: (E[3][LATE],),
         32: (E[2][FINISH],),
         48: (E[3][FINISH],),
     }
@@ -597,29 +594,34 @@
     for step in odd:
         col_landing(step).wait_recv()
     C[1][BEGIN]()
-    for part in (MID, LATE, FINISH):
+    for part in (MID, LATE):
         for band in (R[0], C[0], R[1], C[1]):
             band[part]()
+    R[0][FINISH]()
+    C[0][FINISH]()
+    R[1][FINISH]()
 
     depth = rows.shape[2] * rows.shape[3] * rows.shape[4]
     half = rows.shape[4] // 2
 
-    def multiply(k, last):
+    def multiply(k, blocks, last):
         right = cols[k].reshape(depth // (2 * half), 2 * half, BLOCK_PAD)
         turned = jnp.concatenate([-right[:, half:], right[:, :half]], axis=1)
         right = right.reshape(depth, BLOCK_PAD)
         turned = turned.reshape(depth, BLOCK_PAD)
-        for b in range(2):
+        for b in blocks:
             left = rows[b, k].reshape(depth, BLOCK_PAD)
             for at, side in ((0, right), (1, turned)):
                 part = lax.dot_general(left, side, (((0,), (0,)), ((), ())), preferred_element_type=f32)
+                part = part[:BLOCK, :BLOCK]
                 out[at, b] = (out[at, b] + part) * factor if last else part
 
-    multiply(core, False)
+    multiply(core, (0, 1), False)
+    C[1][FINISH]()
     for b in range(2):
         for i in range(8):
             share(b, 1 - core, i).wait_recv()
-    multiply(1 - core, True)
+    multiply(1 - core, (0, 1), True)
     for step in row_steps:
         for b in range(2):
             row_part(b, step).wait_send()
@@ -642,7 +644,7 @@
     dma = pltpu.SemaphoreType.DMA
     chi = pl.pallas_call(
         functools.partial(chi_kernel, factor),
-        out_shape=jax.ShapeDtypeStruct((2, 2, BLOCK_PAD, BLOCK_PAD), f32),
+        out_shape=jax.ShapeDtypeStruct((2, 2, BLOCK, BLOCK), f32),
         in_specs=[pl.BlockSpec(memory_space=pl.ANY)],
         out_specs=vmem,
         scratch_shapes=[
@@ -663,7 +665,7 @@
         ),
         name="chi_blocks",
     )(d)
-    return chi[:, :, :BLOCK, :BLOCK].reshape(2, 2 * BLOCK, BLOCK)
+    return chi.reshape(2, 2 * BLOCK, BLOCK)
 
 
 def solution(mesh):

time: 306 us -> 293 us (0.958)
  Pallas kernels: 280 us -> 270 us
  local copies, waits for them, and re-layouts: 23.7 us -> 19.2 us
    pallas_call x1, Pallas kernels: 69 us -> 64.1 us  [body(): pl.pallas_call(functools.partial(chi_kernel, factor), out_shape=jax.Shape...]
    pallas_call x1, Pallas kernels: 198 us -> 193 us  [compact(): pl.pallas_call(pair_kernel, out_shape=jax.ShapeDtypeStruct((2, n_occ, n_e...]
    slice x1 -> x0, local copies, waits for them, and re-layouts: 4.56 us -> none  [body(): return chi[:, :, :BLOCK, :BLOCK].reshape(2, 2 * BLOCK, BLOCK)]
where the time goes in v5:
time: 293 us; the launch traced here: 291 us
  Pallas kernels  270 us (92%)
  local copies, waits for them, and re-layouts  19.2 us (7%)
    pallas_call x1, Pallas kernels, compact(): pl.pallas_call(pair_kernel, out_shape=jax.ShapeDtypeStruct((2, n_occ, n_e...  193 us
    pallas_call x1, Pallas kernels, body(): pl.pallas_call(functools.partial(chi_kernel, factor), out_shape=jax.Shape...  64.1 us
    pallas_call x1, Pallas kernels, select(): pl.pallas_call(select_kernel, grid=(blocks,), out_shape=jax.ShapeDtypeStr...  12.8 us

profile of v5, /device:TPU:1, one launch (start us, length us, event | category | flops | bytes accessed | tf_op | source)
XLA Modules:
  0.0 291.0 jit_solution(3058593965966658973)
XLA Ops:
  0.0 1.3 sqrt_multiply_fusion.weight
  1.3 0.9 reshape.23
  2.2 0.2 multiply_subtract_fusion
  2.5 2.6 reshape.24
  5.1 1.1 copy.12
  6.1 1.1 copy.14.occ_in
  7.2 4.3 %reshape.26 = bf16[2,4,2,6,24,3,128]{6,5,4,1,3,2,0:T(4,128)(2,1)S(1)} reshape(bf16[2,4,12,9216]{3,1,2,0:T(4,128)(2,1)} %param.10) | data formatting | bytes 3538944 | tf_op jit(solution)/shard_map/reshape | solution.py:417
  11.5 2.1 copy.13
  13.6 1.4 copy.15.emp_in
  15.0 0.0 copy-start.2
  15.0 193.3 %pair_spectra.1 = bf16[2,4,4,32,512]{4,3,2,1,0:T(8,128)(2,1)} custom-call(f32[4,4]{1,0:T(4,128)} %sqrt_multiply_fusion.weight, bf16[4,2,3,144,128]{4,3,2,1,0:T(8,128)(2,1)} %copy.14.occ_in, bf16[4,2,2,3,144,128]{5,4,3,2,1,0:T(8,128)(2,1)} %copy.15.emp_in, bf16[768,256]{1,0:T(8,128)(2,1)} %constant.30.clone.first, bf16[1024,2304]{1,0:T(8,128)(2,1)} %constant.31.clone.second, ...), custom_call_target="tpu_custom_call" | custom-call | tf_op jit(solution)/shard_map/pair_spectra/pallas_call | solution.py:422
  208.4 0.0 copy-done.2
  208.4 0.0 copy-start
  208.4 1.2 copy-done
  209.6 12.8 %sphere_select.1.d = bf16[16,32,512]{2,1,0:T(8,128)(2,1)S(1)} custom-call(s32[512,1]{1,0:T(8,128)S(1)} %copy-done.2, s32[16,1,512]{2,1,0:T(1,128)S(1)} %broadcast_select_fusion.kxy, s32[16,1,512]{2,1,0:T(1,128)S(1)} %get-tuple-element.5.kz, bf16[1024,512]{1,0:T(8,128)(2,1)S(1)} %bitcast.9), custom_call_target="tpu_custom_call" | custom-call | tf_op jit(solution)/shard_map/sphere_select/pallas_call | solution.py:470
  222.4 0.0 copy-start.1
  222.4 0.8 copy-done.1
  223.2 64.1 %chi_blocks.1 = f32[2,2,500,500]{3,2,1,0:T(8,128)} custom-call(bf16[16,32,512]{2,1,0:T(8,128)(2,1)} %copy-done.1), custom_call_target="tpu_custom_call" | custom-call | tf_op jit(solution)/shard_map/chi_blocks/pallas_call | solution.py:645
  287.3 3.8 %reshape.29 = f32[2,1000,500]{2,1,0:T(8,128)} reshape(f32[2,2,500,500]{3,2,1,0:T(8,128)} %chi_blocks.1) | data formatting | bytes 8000000 | tf_op jit(solution)/shard_map/reshape | solution.py:668
  (2 shorter events, 0.0 us)
Async XLA Ops:
  15.0 193.3 %copy-start.2 = (s32[512,1]{1,0:T(8,128)S(1)}, s32[512,1]{1,0:T(8,128)}, u32[]{:S(2)}) copy-start(s32[512,1]{1,0:T(8,128)} %constant.33.clone.column) | copy-start | bytes 6148
  208.4 1.2 copy-start
  222.4 0.8 copy-start.1

commit v6 on v5

--- a/solution.py
+++ b/solution.py
@@ -21,7 +21,7 @@
 HALF = 256
 KZ = 32
 CHUNK_Y = ((0, 1), (2, 1), (2, 3))
-RING_FIRST = ()
+RING_FIRST = (3,)
 BLOCK = 500
 BLOCK_PAD = 512
 
@@ -295,8 +295,8 @@
         15: (lambda: pass_on(3),),
         17: (E[2][LATE],),
         18: (lambda: shared(3),),
-        23: (E[3][MID],),
-        28: (E[3][LATE],),
+        21: (E[3][MID],),
+        25: (E[3][LATE],),
         32: (E[2][FINISH],),
         48: (E[3][FINISH],),
     }

time: 293 us -> 291 us (level)
  no operation moved by 1% of the time
where the time goes in v6:
time: 291 us; the launch traced here: 289 us
  Pallas kernels  268 us (92%)
  local copies, waits for them, and re-layouts  19.2 us (7%)
    pallas_call x1, Pallas kernels, compact(): pl.pallas_call(pair_kernel, out_shape=jax.ShapeDtypeStruct((2, n_occ, n_e...  192 us
    pallas_call x1, Pallas kernels, body(): pl.pallas_call(functools.partial(chi_kernel, factor), out_shape=jax.Shape...  63.7 us
    pallas_call x1, Pallas kernels, select(): pl.pallas_call(select_kernel, grid=(blocks,), out_shape=jax.ShapeDtypeStr...  12.8 us

profile of v6, /device:TPU:1, one launch (start us, length us, event | category | flops | bytes accessed | tf_op | source)
XLA Modules:
  0.0 289.3 jit_solution(6300545661340205826)
XLA Ops:
  0.0 1.3 sqrt_multiply_fusion.weight
  1.3 0.9 reshape.23
  2.2 0.2 multiply_subtract_fusion
  2.5 2.6 reshape.24
  5.1 1.1 copy.12
  6.1 1.1 copy.14.occ_in
  7.2 4.3 %reshape.26 = bf16[2,4,2,6,24,3,128]{6,5,4,1,3,2,0:T(4,128)(2,1)S(1)} reshape(bf16[2,4,12,9216]{3,1,2,0:T(4,128)(2,1)} %param.10) | data formatting | bytes 3538944 | tf_op jit(solution)/shard_map/reshape | solution.py:417
  11.5 2.1 copy.13
  13.6 1.4 copy.15.emp_in
  15.0 0.0 copy-start.2
  15.0 191.9 %pair_spectra.1 = bf16[2,4,4,32,512]{4,3,2,1,0:T(8,128)(2,1)} custom-call(f32[4,4]{1,0:T(4,128)} %sqrt_multiply_fusion.weight, bf16[4,2,3,144,128]{4,3,2,1,0:T(8,128)(2,1)} %copy.14.occ_in, bf16[4,2,2,3,144,128]{5,4,3,2,1,0:T(8,128)(2,1)} %copy.15.emp_in, bf16[768,256]{1,0:T(8,128)(2,1)} %constant.30.clone.first, bf16[1024,2304]{1,0:T(8,128)(2,1)} %constant.31.clone.second, ...), custom_call_target="tpu_custom_call" | custom-call | tf_op jit(solution)/shard_map/pair_spectra/pallas_call | solution.py:422
  207.0 0.0 copy-done.2
  207.0 0.0 copy-start
  207.0 1.2 copy-done
  208.2 12.8 %sphere_select.1.d = bf16[16,32,512]{2,1,0:T(8,128)(2,1)S(1)} custom-call(s32[512,1]{1,0:T(8,128)S(1)} %copy-done.2, s32[16,1,512]{2,1,0:T(1,128)S(1)} %broadcast_select_fusion.kxy, s32[16,1,512]{2,1,0:T(1,128)S(1)} %get-tuple-element.5.kz, bf16[1024,512]{1,0:T(8,128)(2,1)S(1)} %bitcast.9), custom_call_target="tpu_custom_call" | custom-call | tf_op jit(solution)/shard_map/sphere_select/pallas_call | solution.py:470
  221.0 0.0 copy-start.1
  221.0 0.8 copy-done.1
  221.8 63.7 %chi_blocks.1 = f32[2,2,500,500]{3,2,1,0:T(8,128)} custom-call(bf16[16,32,512]{2,1,0:T(8,128)(2,1)} %copy-done.1), custom_call_target="tpu_custom_call" | custom-call | tf_op jit(solution)/shard_map/chi_blocks/pallas_call | solution.py:645
  285.6 3.8 %reshape.29 = f32[2,1000,500]{2,1,0:T(8,128)} reshape(f32[2,2,500,500]{3,2,1,0:T(8,128)} %chi_blocks.1) | data formatting | bytes 8000000 | tf_op jit(solution)/shard_map/reshape | solution.py:668
  (2 shorter events, 0.0 us)
Async XLA Ops:
  15.0 191.9 %copy-start.2 = (s32[512,1]{1,0:T(8,128)S(1)}, s32[512,1]{1,0:T(8,128)}, u32[]{:S(2)}) copy-start(s32[512,1]{1,0:T(8,128)} %constant.33.clone.column) | copy-start | bytes 6148
  207.0 1.2 copy-start
  221.0 0.8 copy-start.1
